TPU v7x, 128 devices: a whole 4x4x4 slice. The times are simulated.
128 devices in a mesh: wide: 16 (over z, y), narrow: 8 (over x, core).
Axes of the slice: x: 4, y: 4, z: 4, core: 2. Of those that a mesh axis runs over, the one named last changes fastest.
Arguments:
- material_flow_vector: float32 [3, 256, 256, 512], P(None, 'wide', 'narrow'), may hold values from -6 to 6
- tool_push_density: float32 [3, 256, 256, 512], P(None, 'wide', 'narrow'), may hold values from -6 to 6
- tool_warmth_excess: float32 [256, 256, 512], P('wide', 'narrow'), may hold values from 0.7 to 1.3
- substrate_warmth_excess: float32 [256, 256, 128], P('wide', 'narrow'), may hold values from -6 to 6
- spread_coefficient: float32 [256, 256, 128], P('wide', 'narrow'), may hold values from 0.02 to 0.08
- source_owner_sheet: int32 [262144, 1], P(('wide', 'narrow')), may hold values from 0 to 15; in each aligned block of 2048 rows (0 to 2047, 2048 to 4095, ...) at most 384 rows name the same one
- source_part_line: int32 [262144], P(('wide', 'narrow')), may hold values from 0 to 511
Outputs:
- corrected_flow_vector: float32 [3, 256, 256, 512], P(None, 'wide', 'narrow')
- part_out: float32 [256, 256, 128], P('wide', 'narrow')
Inputs may be any that keep to these rules, and one draw needn't show every extreme that they name: `source_owner_sheet`: among the 2048 blocks of one device, no slab is named by more than 384 of them.
All inputs are finite; a program needn't handle non-finite values.
Results may differ from a plain program's by a relative error of at most 0.00012.
Values sent between devices are 32-bit elements; how exact they have to be, the bound alone decides.
A program may use at most 128 MiB of HBM per device.

v0:
```python
import functools
import math

import jax
import jax.numpy as jnp
import ml_dtypes
import numpy as np
from jax import lax
from jax.experimental import pallas as pl
from jax.experimental.pallas import tpu as pltpu
from jax.sharding import PartitionSpec as P

STEPS = 3
MESH = pl.DeviceIdType.MESH
F32 = jnp.float32
BF16 = jnp.bfloat16
VM = pl.BlockSpec(memory_space=pltpu.VMEM)

time_step = 0.15
rate_base = 0.5
zener_energy = 4.0
stress_exponent = 5.0
penalty = 0.001
dissipation_factor = 0.1
GROUPS = 2


def shifted(x, axis, up, wrap):
    size = lax.axis_size(axis)
    pairs = [(i, (i + 1) % size) for i in range(size if wrap else size - 1)]
    if not up:
        pairs = [(j, i) for i, j in pairs]
    return lax.ppermute(x, axis, pairs)


def with_halo(x, sides, width, wrap):
    for axis, dim in sides:
        length = x.shape[dim]
        last = lax.slice_in_dim(x, length - width, length, axis=dim)
        initial = lax.slice_in_dim(x, 0, width, axis=dim)
        before = shifted(last, axis, True, wrap)
        after = shifted(initial, axis, False, wrap)
        x = jnp.concatenate([before, x, after], axis=dim)
    return x


PAD = 8
STRIP = 8


def flow_kernel(
    n_wide, n_narrow,
    vel_in, push_in, warmth_in,
    mom, div, heat,
    velp, provp, mup0, mup1, lz, push,
    vel_ys, vel_yr, mu_ys0, mu_yr0, prov_ys, prov_yr, mu_ys1, mu_yr1, mom_ys, mom_yr, mom_xr,
    load_sem, h_send, h_recv,
):
    w = lax.axis_index("wide")
    n = lax.axis_index("narrow")
    _, planes, rows, n_z = vel_in.shape
    strips = rows // STRIP
    wide_to = (lax.rem(w + n_wide - 1, n_wide), lax.rem(w + 1, n_wide))
    narrow_to = (lax.rem(n + n_narrow - 1, n_narrow), lax.rem(n + 1, n_narrow))
    body = pl.ds(PAD, rows)

    barrier = pltpu.get_barrier_semaphore()
    for side in (0, 1):
        pl.semaphore_signal(barrier, inc=1, device_id=(wide_to[side], n), device_id_type=MESH)
        pl.semaphore_signal(barrier, inc=1, device_id=(w, narrow_to[side]), device_id_type=MESH)

    loads = [
        pltpu.make_async_copy(vel_in, velp.at[:, pl.ds(1, planes), body], load_sem.at[0]),
        pltpu.make_async_copy(warmth_in, lz, load_sem.at[1]),
        pltpu.make_async_copy(push_in, push, load_sem.at[2]),
    ]
    for load in loads:
        load.start()

    def wide_copy(e, side, source, target):
        return pltpu.make_async_remote_copy(
            src_ref=source, dst_ref=target,
            send_sem=h_send.at[e, side], recv_sem=h_recv.at[e, 1 - side],
            device_id=(wide_to[side], n), device_id_type=MESH,
        )

    def narrow_copy(e, side, sends, lands):
        return pltpu.make_async_remote_copy(
            src_ref=sends.at[side], dst_ref=lands.at[1 - side],
            send_sem=h_send.at[e, 2 + side], recv_sem=h_recv.at[e, 3 - side],
            device_id=(w, narrow_to[side]), device_id_type=MESH,
        )

    def x_pair(e, field, lead=()):
        return [
            wide_copy(e, 0, field.at[lead + (1, body)], field.at[lead + (planes + 1, body)]),
            wide_copy(e, 1, field.at[lead + (planes, body)], field.at[lead + (0, body)]),
        ]

    def y_pair(e, sends, lands):
        return [narrow_copy(e, side, sends, lands) for side in (0, 1)]

    def all_x(action, first=0, last=None):
        def step(x, c):
            action(x)
            return c

        lax.fori_loop(first, planes if last is None else last, step, 0)

    def y_fill(field, lands, comps):
        def fill(x):
            here = pl.ds(x, 1)
            if comps is None:
                field[x + 1, PAD - 1:PAD] = lands[0, here]
                field[x + 1, PAD + rows:PAD + rows + 1] = lands[1, here]
                return
            for i, c in enumerate(comps):
                field[c, x + 1, PAD - 1:PAD] = lands[0, i, here]
                field[c, x + 1, PAD + rows:PAD + rows + 1] = lands[1, i, here]

        all_x(fill)

    def z_ahead(a):
        return pltpu.roll(a, n_z - 1, 1)

    def z_behind(a):
        return pltpu.roll(a, 1, 1)

    loads[0].wait()

    def vel_rows(x):
        for c in range(3):
            vel_ys[0, c, pl.ds(x, 1)] = velp[c, x + 1, PAD:PAD + 1]
            vel_ys[1, c, pl.ds(x, 1)] = velp[c, x + 1, PAD + rows - 1:PAD + rows]

    all_x(vel_rows)
    pl.semaphore_wait(barrier, 4)
    every = slice(None)
    vel_x = x_pair(0, velp, (every,))
    vel_y = y_pair(0, vel_ys, vel_yr)
    for copy in vel_x + vel_y:
        copy.start()
    loads[1].wait()

    def zener_log(x):
        lz[x] = (zener_energy / stress_exponent) * (1.0 / lz[x] - 1.0)

    all_x(zener_log)
    loads[2].wait()

    def excess(src, x, r):
        here = slice(PAD + STRIP * r, PAD + STRIP * (r + 1))
        up = slice(PAD + STRIP * r + 1, PAD + STRIP * (r + 1) + 1)
        down = slice(PAD + STRIP * r - 1, PAD + STRIP * (r + 1) - 1)
        dx = [src[c, x + 2, here] - src[c, x, here] for c in range(3)]
        dy = [src[c, x + 1, up] - src[c, x + 1, down] for c in range(3)]
        mid = [src[c, x + 1, here] for c in range(3)]
        dz = [z_ahead(m) - z_behind(m) for m in mid]
        xy, xz, yz = dy[0] + dx[1], dz[0] + dx[2], dz[1] + dy[2]
        diagonal = dx[0] * dx[0] + dy[1] * dy[1] + dz[2] * dz[2]
        return 0.5 * diagonal + 0.25 * (xy * xy + xz * xz + yz * yz)

    def mu_plane(src, mup, ys, with_heat):
        def plane(x):
            for r in range(strips):
                part = slice(STRIP * r, STRIP * (r + 1))
                extra = excess(src, x, r)
                rate_sq = extra + rate_base**2
                v = jnp.exp((0.5 / stress_exponent) * jnp.log(rate_sq) + lz[x, part])
                mu = jnp.log(v + jnp.sqrt(v * v + 1.0)) * lax.rsqrt(rate_sq) * (1.0 / 3.0)
                mup[x + 1, PAD + STRIP * r:PAD + STRIP * (r + 1)] = mu
                if r == 0:
                    ys[0, pl.ds(x, 1)] = mu[0:1]
                if r == strips - 1:
                    ys[1, pl.ds(x, 1)] = mu[STRIP - 1:]
                if with_heat:
                    h = mu * extra
                    to = pl.ds(pl.multiple_of(x * rows + STRIP * r, STRIP), STRIP)
                    for m in range(n_z // 128):
                        heat[m, to] = h[:, 128 * m:128 * (m + 1)]

        return plane

    def advance_plane(mup, final):
        def plane(x):
            for r in range(strips):
                part = slice(STRIP * r, STRIP * (r + 1))
                here = slice(PAD + STRIP * r, PAD + STRIP * (r + 1))
                up = slice(PAD + STRIP * r + 1, PAD + STRIP * (r + 1) + 1)
                down = slice(PAD + STRIP * r - 1, PAD + STRIP * (r + 1) - 1)
                m = mup[x + 1, here]
                m_xp = m + mup[x + 2, here]
                m_xm = m + mup[x, here]
                m_yp = m + mup[x + 1, up]
                m_ym = m + mup[x + 1, down]
                m_z = m + z_ahead(m)
                for c in range(3):
                    u = velp[c, x + 1, here]
                    flux = m_z * (z_ahead(u) - u)
                    total = flux - z_behind(flux)
                    total += m_xp * (velp[c, x + 2, here] - u) - m_xm * (u - velp[c, x, here])
                    total += m_yp * (velp[c, x + 1, up] - u) - m_ym * (u - velp[c, x + 1, down])
                    new = u + (0.5 * time_step) * total + time_step * push[c, x, part]
                    provp[c, x + 1, here] = new
                    if final:
                        mom[c, x, part] = new
                        if c == 1:
                            if r == 0:
                                mom_ys[0, pl.ds(x, 1)] = new[0:1]
                            if r == strips - 1:
                                mom_ys[1, pl.ds(x, 1)] = new[STRIP - 1:]
                    else:
                        if r == 0:
                            prov_ys[0, c, pl.ds(x, 1)] = new[0:1]
                        if r == strips - 1:
                            prov_ys[1, c, pl.ds(x, 1)] = new[STRIP - 1:]

        return plane

    def stage(action, arriving_x, arriving_y, fill):
        for copy in arriving_y:
            copy.wait_recv()
        fill()
        all_x(action, 1, planes - 1)
        for copy in arriving_x:
            copy.wait_recv()
        all_x(lambda i: action(i * (planes - 1)), 0, 2)

    stage(mu_plane(velp, mup0, mu_ys0, False), vel_x, vel_y,
          lambda: y_fill(velp, vel_yr, (0, 1, 2)))
    mu_x0 = x_pair(1, mup0)
    mu_y0 = y_pair(1, mu_ys0, mu_yr0)
    for copy in mu_x0 + mu_y0:
        copy.start()
    stage(advance_plane(mup0, False), mu_x0, mu_y0, lambda: y_fill(mup0, mu_yr0, None))
    prov_x = x_pair(2, provp, (every,))
    prov_y = y_pair(2, prov_ys, prov_yr)
    for copy in prov_x + prov_y:
        copy.start()
    stage(mu_plane(provp, mup1, mu_ys1, True), prov_x, prov_y,
          lambda: y_fill(provp, prov_yr, (0, 1, 2)))
    mu_x1 = x_pair(3, mup1)
    mu_y1 = y_pair(3, mu_ys1, mu_yr1)
    for copy in mu_x1 + mu_y1:
        copy.start()
    for copy in prov_x + prov_y:
        copy.wait_send()
    stage(advance_plane(mup1, True), mu_x1, mu_y1, lambda: y_fill(mup1, mu_yr1, None))
    mom_x = [
        wide_copy(4, 0, mom.at[0, 0], mom_xr.at[1]),
        wide_copy(4, 1, mom.at[0, planes - 1], mom_xr.at[0]),
    ]
    mom_y = y_pair(4, mom_ys, mom_yr)
    for copy in mom_x + mom_y:
        copy.start()
    for copy in vel_x + vel_y + mu_x0 + mu_y0 + mu_x1 + mu_y1:
        copy.wait_send()

    def fill_rows():
        def fill(x):
            here = pl.ds(x, 1)
            provp[1, x + 1, PAD - 1:PAD] = mom_yr[0, here]
            provp[1, x + 1, PAD + rows:PAD + rows + 1] = mom_yr[1, here]

        all_x(fill)

    def div_plane(x):
        for r in range(strips):
            part = slice(STRIP * r, STRIP * (r + 1))
            here = slice(PAD + STRIP * r, PAD + STRIP * (r + 1))
            up = slice(PAD + STRIP * r + 1, PAD + STRIP * (r + 1) + 1)
            down = slice(PAD + STRIP * r - 1, PAD + STRIP * (r + 1) - 1)
            u = provp[2, x + 1, here]
            total = provp[0, x + 2, here] - provp[0, x, here]
            total += provp[1, x + 1, up] - provp[1, x + 1, down]
            div[x, part] = 0.5 * (total + (z_ahead(u) - z_behind(u)))

    for copy in mom_y:
        copy.wait_recv()
    fill_rows()
    all_x(div_plane, 1, planes - 1)
    for copy in mom_x:
        copy.wait_recv()
    provp[0, 0, body] = mom_xr[0]
    provp[0, planes + 1, body] = mom_xr[1]
    all_x(lambda i: div_plane(i * (planes - 1)), 0, 2)
    for copy in mom_x + mom_y:
        copy.wait_send()


def flow(velocity, push, warmth):
    n_wide, n_narrow = lax.axis_size("wide"), lax.axis_size("narrow")
    _, planes, rows, n_z = velocity.shape
    padded = (planes + 2, PAD + rows + PAD, n_z)
    line = (2, planes, n_z)
    lines = (2, 3, planes, n_z)
    any_space = pl.BlockSpec(memory_space=pl.ANY)
    shapes = [(3,) + padded, (3,) + padded, padded, padded, (planes, rows, n_z), velocity.shape]
    shapes += [lines, lines, line, line, lines, lines, line, line, line, line, (2, rows, n_z)]
    dma = pltpu.SemaphoreType.DMA
    return pl.pallas_call(
        functools.partial(flow_kernel, n_wide, n_narrow),
        out_shape=[
            jax.ShapeDtypeStruct(velocity.shape, F32),
            jax.ShapeDtypeStruct((planes, rows, n_z), F32),
            jax.ShapeDtypeStruct((n_z // 128, planes * rows, 128), F32),
        ],
        in_specs=[any_space] * 3,
        out_specs=[VM] * 3,
        scratch_shapes=[pltpu.VMEM(shape, F32) for shape in shapes]
        + [dma((3,)), dma((5, 4)), dma((5, 4))],
        compiler_params=pltpu.CompilerParams(
            collective_id=2, has_side_effects=True, vmem_limit_bytes=48 * 2**20
        ),
        name="flow",
    )(velocity, push, warmth)


def gather_kernel(target, heat, out, other):
    out[...] = jnp.zeros_like(out)
    other[...] = jnp.zeros_like(other)
    depth = heat.shape[0]

    def cell(i, c):
        for m in range(depth):
            into = out if m % 2 == 0 else other
            row = pl.ds(target[i * depth + m], 1)
            into[row] = into[row] + heat[m, pl.ds(i, 1)]
        return c

    lax.fori_loop(0, heat.shape[1], cell, 0, unroll=4)
    step = 256

    def join(i, c):
        here = pl.ds(pl.multiple_of(i * step, step), step)
        out[here] = out[here] + other[here]
        return c

    lax.fori_loop(0, out.shape[0] // step, join, 0)


def slab_heat(target, heat, lines):
    return pl.pallas_call(
        gather_kernel,
        out_shape=jax.ShapeDtypeStruct((lines, 128), F32),
        in_specs=[pl.BlockSpec(memory_space=pltpu.SMEM), VM],
        out_specs=VM,
        scratch_shapes=[pltpu.VMEM((lines, 128), F32)],
        compiler_params=pltpu.CompilerParams(vmem_limit_bytes=24 * 2**20),
        name="slab_heat",
    )(target, heat)


def real_basis(length):
    cells = np.arange(length, dtype=np.float64)
    rows = [np.full(length, 1.0 / math.sqrt(length)), (-1.0) ** cells / math.sqrt(length)]
    waves = [0, length // 2]
    for k in range(1, length // 2):
        angle = 2.0 * math.pi * k * cells / length
        rows.append(np.cos(angle) * math.sqrt(2.0 / length))
        rows.append(np.sin(angle) * math.sqrt(2.0 / length))
        waves += [k, k]
    waves = np.array(waves)
    symbol = np.sin(2.0 * math.pi * (waves % (length // 2)) / length) ** 2
    return np.stack(rows), symbol


def split_table(table):
    high = table.astype(np.float32).astype(ml_dtypes.bfloat16)
    low = (table - high.astype(np.float64)).astype(np.float32).astype(ml_dtypes.bfloat16)
    return [high, low]


def pressure_tables(n_y, n_z, n_narrow):
    basis_z, symbol_z = real_basis(n_z)
    basis_y, symbol_y = real_basis(n_y)
    forward = basis_z.T
    swapped = forward.reshape(n_z, n_z // 128, 2, 64)[:, :, ::-1].reshape(n_z, n_z)
    tables = []
    for table in (forward, swapped, forward.T, swapped.T, basis_y, basis_y.T):
        tables += split_table(np.ascontiguousarray(table))
    s_y = np.broadcast_to(symbol_y[:, None], (n_y, 128)).astype(np.float32)
    s_z = np.tile(symbol_z.reshape(n_narrow, 1, 64), (1, 8, 2)).astype(np.float32)
    return tables + [s_y, s_z]


def split_value(x):
    high = x.astype(BF16)
    return high, (x - high.astype(F32)).astype(BF16)


def dot_left(x, high, low):
    x_high, x_low = split_value(x)
    dot = functools.partial(jnp.dot, preferred_element_type=F32)
    return dot(x_high, high) + (dot(x_high, low) + dot(x_low, high))


def dot_right(high, low, x):
    x_high, x_low = split_value(x)
    dot = functools.partial(jnp.dot, preferred_element_type=F32)
    return dot(high, x_high) + (dot(low, x_high) + dot(high, x_low))


def pressure_kernel(
    n_wide, n_narrow,
    div, fe_h, fe_l, fo_h, fo_l, ie_h, ie_l, io_h, io_l, cy_h, cy_l, iy_h, iy_l, s_y, s_z,
    press, y_halo,
    zsend, rbuf, ubuf, vsend, zrecv, rtab, mom, mrecv, absend, ab, xrecv, yrecv, ysend,
    nf_send, nf_recv, nb_send, nb_recv, wf_send, wf_recv, wb_send, wb_recv, h_send, h_recv,
):
    w = lax.axis_index("wide")
    n = lax.axis_index("narrow")
    xps, _, rows, n_z = div.shape
    n_y = s_y.shape[0]
    per = xps // GROUPS
    chunk_rows = n_y // n_wide

    def across(k):
        return lax.rem(n + k, n_narrow)

    def along(k):
        return lax.rem(w + k, n_wide)

    barrier = pltpu.get_barrier_semaphore()

    def greet_n(k, c):
        pl.semaphore_signal(barrier, inc=1, device_id=(w, across(k)), device_id_type=MESH)
        return c

    def greet_w(k, c):
        pl.semaphore_signal(barrier, inc=1, device_id=(along(k), n), device_id_type=MESH)
        return c

    lax.fori_loop(1, n_narrow, greet_n, 0)
    lax.fori_loop(1, n_wide, greet_w, 0)

    lane = lax.broadcasted_iota(jnp.int32, (per * rows, 128), 1)
    low_half = lane < 64

    def forward_copy(g, k):
        to = across(k)
        return pltpu.make_async_remote_copy(
            src_ref=zsend.at[to, pl.ds(g * per, per)],
            dst_ref=rbuf.at[pl.ds(g * per, per), pl.ds(pl.multiple_of(n * rows, rows), rows)],
            send_sem=nf_send.at[g, k],
            recv_sem=nf_recv.at[g, k],
            device_id=(w, to),
            device_id_type=MESH,
        )

    def forward_arrival(g, k):
        source = across(n_narrow - k)
        here = rbuf.at[pl.ds(g * per, per), pl.ds(pl.multiple_of(source * rows, rows), rows)]
        return pltpu.make_async_remote_copy(
            src_ref=here, dst_ref=here, send_sem=nf_send.at[g, k], recv_sem=nf_recv.at[g, k],
            device_id=(w, source), device_id_type=MESH,
        )

    for g in range(GROUPS):
        even = div[g * per:(g + 1) * per, 0].reshape(per * rows, n_z)
        odd = div[g * per:(g + 1) * per, 1].reshape(per * rows, n_z)
        even = dot_left(even, fe_h[...], fe_l[...])
        odd = dot_left(odd, fo_h[...], fo_l[...])
        for m in range(n_z // 128):
            e = even[:, 128 * m:128 * (m + 1)]
            o = odd[:, 128 * m:128 * (m + 1)]
            first = jnp.where(low_half, e, o)
            second = jnp.where(low_half, o, e)
            zsend[2 * m, g * per:(g + 1) * per] = first.reshape(per, rows, 128)
            zsend[2 * m + 1, g * per:(g + 1) * per] = second.reshape(per, rows, 128)
        if g == 0:
            pl.semaphore_wait(barrier, n_narrow - 1 + n_wide - 1)

        def launch(k, c):
            forward_copy(g, k).start()
            return c

        lax.fori_loop(1, n_narrow, launch, 0)

    s = s_y[...] + s_z[n][0:1, :] + penalty
    root = jnp.sqrt(s * (1.0 + s))
    rtab[0] = 1.0 / (1.0 + 2.0 * s + 2.0 * root)
    rtab[1] = -1.0 / root

    for g in range(GROUPS):
        span = slice(g * per, (g + 1) * per)
        rbuf[span, pl.ds(pl.multiple_of(n * rows, rows), rows)] = zsend[n, span]

        def arrive(k, c):
            forward_arrival(g, k).wait_recv()
            return c

        lax.fori_loop(1, n_narrow, arrive, 0)
        lines = jnp.concatenate([rbuf[xp] for xp in range(g * per, (g + 1) * per)], axis=1)
        lines = dot_right(cy_h[...], cy_l[...], lines)
        for i in range(per):
            ubuf[g * per + i] = lines[:, 128 * i:128 * (i + 1)]

    block = 16

    def moments(i, c):
        here = pl.ds(pl.multiple_of(i * block, block), block)
        r = rtab[0, here]
        f = ubuf[0, here]
        b = ubuf[xps - 1, here]
        for xp in range(1, xps):
            f = f * r + ubuf[xp, here]
            b = b * r + ubuf[xps - 1 - xp, here]
        mom[0, here] = f
        mom[1, here] = b
        return c

    lax.fori_loop(0, n_y // block, moments, 0)

    def chunk(index):
        return pl.ds(pl.multiple_of(index * chunk_rows, chunk_rows), chunk_rows)

    def out_copy(k):
        to = along(k)
        return pltpu.make_async_remote_copy(
            src_ref=mom.at[:, chunk(to)], dst_ref=mrecv.at[w],
            send_sem=wf_send.at[k], recv_sem=wf_recv.at[k],
            device_id=(to, n), device_id_type=MESH,
        )

    def out_arrival(k):
        here = mrecv.at[along(n_wide - k)]
        return pltpu.make_async_remote_copy(
            src_ref=here, dst_ref=here, send_sem=wf_send.at[k], recv_sem=wf_recv.at[k],
            device_id=(along(n_wide - k), n), device_id_type=MESH,
        )

    def back_copy(k):
        to = along(k)
        return pltpu.make_async_remote_copy(
            src_ref=absend.at[to], dst_ref=ab.at[:, chunk(w)],
            send_sem=wb_send.at[k], recv_sem=wb_recv.at[k],
            device_id=(to, n), device_id_type=MESH,
        )

    def back_arrival(k):
        here = ab.at[:, chunk(along(n_wide - k))]
        return pltpu.make_async_remote_copy(
            src_ref=here, dst_ref=here, send_sem=wb_send.at[k], recv_sem=wb_recv.at[k],
            device_id=(along(n_wide - k), n), device_id_type=MESH,
        )

    def each(count, action):
        def body(k, c):
            action(k)
            return c

        lax.fori_loop(1, count, body, 0)

    each(n_wide, lambda k: out_copy(k).start())
    mrecv[w] = mom[:, chunk(w)]
    r = rtab[0, chunk(w)]
    q = r
    for _ in range(int(math.log2(xps))):
        q = q * q
    total = q
    for _ in range(int(math.log2(n_wide))):
        total = total * total
    closing = 1.0 / (1.0 - total)
    each(n_wide, lambda k: out_arrival(k).wait_recv())
    f = mrecv[0, 0]
    b = mrecv[n_wide - 1, 1]
    for j in range(1, n_wide):
        f = f * q + mrecv[j, 0]
        b = b * q + mrecv[n_wide - 1 - j, 1]
    f = f * closing
    b = b * closing
    for j in range(n_wide):
        absend[j, 0] = f
        absend[n_wide - 1 - j, 1] = b
        f = f * q + mrecv[j, 0]
        b = b * q + mrecv[n_wide - 1 - j, 1]
    each(n_wide, lambda k: back_copy(k).start())
    ab[:, chunk(w)] = absend[w]
    each(n_wide, lambda k: back_arrival(k).wait_recv())

    def solve(i, c):
        here = pl.ds(pl.multiple_of(i * block, block), block)
        r = rtab[0, here]
        scale = rtab[1, here]
        f = ab[0, here]
        b = ab[1, here]
        behind = []
        for xp in range(xps - 1, -1, -1):
            rb = b * r
            behind.append(rb)
            b = rb + ubuf[xp, here]
        for xp in range(xps):
            f = f * r + ubuf[xp, here]
            ubuf[xp, here] = scale * (f + behind[xps - 1 - xp])
        return c

    lax.fori_loop(0, n_y // block, solve, 0)

    def backward_copy(g, k):
        to = across(k)
        return pltpu.make_async_remote_copy(
            src_ref=vsend.at[to, pl.ds(g * per, per)],
            dst_ref=zrecv.at[n, pl.ds(g * per, per)],
            send_sem=nb_send.at[g, k],
            recv_sem=nb_recv.at[g, k],
            device_id=(w, to),
            device_id_type=MESH,
        )

    def backward_arrival(g, k):
        source = across(n_narrow - k)
        here = zrecv.at[source, pl.ds(g * per, per)]
        return pltpu.make_async_remote_copy(
            src_ref=here, dst_ref=here, send_sem=nb_send.at[g, k], recv_sem=nb_recv.at[g, k],
            device_id=(w, source), device_id_type=MESH,
        )

    for g in range(GROUPS):
        span = slice(g * per, (g + 1) * per)
        lines = jnp.concatenate([ubuf[xp] for xp in range(g * per, (g + 1) * per)], axis=1)
        lines = dot_right(iy_h[...], iy_l[...], lines)
        for to in range(n_narrow):
            for i in range(per):
                vsend[to, g * per + i] = lines[to * rows:(to + 1) * rows, 128 * i:128 * (i + 1)]
        each(n_narrow, lambda k: backward_copy(g, k).start())
        zrecv[n, span] = vsend[n, span]

    wide_to = {0: along(n_wide - 1), 1: along(1)}
    narrow_to = {0: across(n_narrow - 1), 1: across(1)}

    def x_halo(side):
        source = 2 * xps if side else 1
        return pltpu.make_async_remote_copy(
            src_ref=press.at[source], dst_ref=xrecv.at[1 - side],
            send_sem=h_send.at[side], recv_sem=h_recv.at[1 - side],
            device_id=(wide_to[side], n), device_id_type=MESH,
        )

    def y_halo_copy(side):
        return pltpu.make_async_remote_copy(
            src_ref=ysend.at[side], dst_ref=yrecv.at[1 - side],
            send_sem=h_send.at[2 + side], recv_sem=h_recv.at[3 - side],
            device_id=(w, narrow_to[side]), device_id_type=MESH,
        )

    for g in range(GROUPS):
        each(n_narrow, lambda k: backward_arrival(g, k).wait_recv())
        evens, odds = [], []
        for m in range(n_z // 128):
            first = zrecv[2 * m, g * per:(g + 1) * per].reshape(per * rows, 128)
            second = zrecv[2 * m + 1, g * per:(g + 1) * per].reshape(per * rows, 128)
            evens.append(jnp.where(low_half, first, second))
            odds.append(jnp.where(low_half, second, first))
        even = dot_left(jnp.concatenate(evens, axis=1), ie_h[...], ie_l[...])
        odd = dot_left(jnp.concatenate(odds, axis=1), io_h[...], io_l[...])
        for i in range(per):
            for parity, part in ((0, even), (1, odd)):
                x = 2 * (g * per + i) + parity
                plane = part[i * rows:(i + 1) * rows]
                press[x + 1] = plane
                ysend[0, x] = plane[0]
                ysend[1, x] = plane[rows - 1]
        if g == 0:
            x_halo(0).start()
    x_halo(1).start()
    y_halo_copy(0).start()
    y_halo_copy(1).start()

    for g in range(GROUPS):
        each(n_narrow, lambda k: forward_copy(g, k).wait_send())
        each(n_narrow, lambda k: backward_copy(g, k).wait_send())
    each(n_wide, lambda k: out_copy(k).wait_send())
    each(n_wide, lambda k: back_copy(k).wait_send())
    for side in (0, 1):
        x_halo(side).wait()
        y_halo_copy(side).wait()
    press[0] = xrecv[0]
    press[2 * xps + 1] = xrecv[1]
    y_halo[...] = yrecv[...]


def solve_pressure(divergence):
    n_wide, n_narrow = lax.axis_size("wide"), lax.axis_size("narrow")
    x_local, rows, n_z = divergence.shape
    n_y = rows * n_narrow
    xps = x_local // 2
    tables = [jnp.asarray(t) for t in pressure_tables(n_y, n_z, n_narrow)]
    dma = pltpu.SemaphoreType.DMA
    field = (xps, n_y, 128)
    turned = (n_narrow, xps, rows, 128)
    chunk_rows = n_y // n_wide
    return pl.pallas_call(
        functools.partial(pressure_kernel, n_wide, n_narrow),
        out_shape=[
            jax.ShapeDtypeStruct((x_local + 2, rows, n_z), F32),
            jax.ShapeDtypeStruct((2, x_local, n_z), F32),
        ],
        in_specs=[VM] * (1 + len(tables)),
        out_specs=[VM, VM],
        scratch_shapes=[
            pltpu.VMEM(turned, F32),
            pltpu.VMEM(field, F32),
            pltpu.VMEM(field, F32),
            pltpu.VMEM(turned, F32),
            pltpu.VMEM(turned, F32),
            pltpu.VMEM((2, n_y, 128), F32),
            pltpu.VMEM((2, n_y, 128), F32),
            pltpu.VMEM((n_wide, 2, chunk_rows, 128), F32),
            pltpu.VMEM((n_wide, 2, chunk_rows, 128), F32),
            pltpu.VMEM((2, n_y, 128), F32),
            pltpu.VMEM((2, rows, n_z), F32),
            pltpu.VMEM((2, x_local, n_z), F32),
            pltpu.VMEM((2, x_local, n_z), F32),
            dma((GROUPS, n_narrow)),
            dma((GROUPS, n_narrow)),
            dma((GROUPS, n_narrow)),
            dma((GROUPS, n_narrow)),
            dma((n_wide,)),
            dma((n_wide,)),
            dma((n_wide,)),
            dma((n_wide,)),
            dma((4,)),
            dma((4,)),
        ],
        compiler_params=pltpu.CompilerParams(
            collective_id=1, has_side_effects=True, vmem_limit_bytes=40 * 2**20
        ),
        name="pressure",
    )(divergence.reshape(xps, 2, rows, n_z), *tables)


def y_step(plane, before, after, ahead):
    rows = plane.shape[0]
    row = lax.broadcasted_iota(jnp.int32, plane.shape, 0)
    if ahead:
        return jnp.where(row == rows - 1, after, pltpu.roll(plane, rows - 1, 0))
    return jnp.where(row == 0, before, pltpu.roll(plane, 1, 0))


def project_kernel(press, y_halo, current, out):
    step = pl.program_id(0)
    n_z = press.shape[2]
    for i in range(current.shape[1]):
        x = step * current.shape[1] + i
        p = press[x + 1]
        before = y_halo[0, pl.ds(x, 1)]
        after = y_halo[1, pl.ds(x, 1)]
        out[0, i] = current[0, i] - (press[x + 2] - press[x]) * 0.5
        out[1, i] = current[1, i] - 0.5 * (
            y_step(p, before, after, True) - y_step(p, before, after, False)
        )
        out[2, i] = current[2, i] - 0.5 * (pltpu.roll(p, n_z - 1, 1) - pltpu.roll(p, 1, 1))


def project(current, divergence):
    press, y_halo = solve_pressure(divergence)
    _, x_local, rows, n_z = current.shape
    planes = 2
    spec = pl.BlockSpec((3, planes, rows, n_z), lambda i: (0, i, 0, 0))
    return pl.pallas_call(
        project_kernel,
        grid=(x_local // planes,),
        out_shape=jax.ShapeDtypeStruct(current.shape, F32),
        in_specs=[VM, VM, spec],
        out_specs=spec,
        compiler_params=pltpu.CompilerParams(vmem_limit_bytes=20 * 2**20),
        name="projection",
    )(press, y_halo, current)


def conduct(thermal_profile, spread_wide):
    sides = (("wide", 0), ("narrow", 1))
    t = with_halo(thermal_profile, sides, STEPS, False)
    coefficient = spread_wide
    for _ in range(STEPS):
        center = t[1:-1, 1:-1]
        coefficient = coefficient[1:-1, 1:-1]
        around = t[2:, 1:-1] + t[:-2, 1:-1] + t[1:-1, 2:] + t[1:-1, :-2]
        ahead = jnp.pad(center[:, :, 1:], ((0, 0), (0, 0), (0, 1)))
        behind = jnp.pad(center[:, :, :-1], ((0, 0), (0, 0), (1, 0)))
        t = center + coefficient * (around + ahead + behind - 6.0 * center)
    return t


def per_device(
    material_flow_vector,
    tool_push_density,
    tool_warmth_excess,
    substrate_warmth_excess,
    spread_coefficient,
    source_owner_sheet,
    source_part_line,
):
    current, divergence, heat = flow(material_flow_vector, tool_push_density, tool_warmth_excess)
    corrected_flow_vector = project(current, divergence)
    spread_wide = with_halo(spread_coefficient, (("wide", 0), ("narrow", 1)), STEPS, False)
    slab_ids = source_owner_sheet[:, 0]
    slab_count = lax.axis_size("wide")
    component_lines = substrate_warmth_excess.shape[0] * substrate_warmth_excess.shape[1]
    target = slab_ids * component_lines + source_part_line
    partial_value = slab_heat(target, heat, slab_count * component_lines)
    substrate_energy_input = lax.psum_scatter(
        partial_value.reshape(slab_count, component_lines, 128),
        "wide",
        scatter_dimension=0,
        tiled=True,
    )
    thermal_profile = substrate_warmth_excess + dissipation_factor * substrate_energy_input.reshape(
        substrate_warmth_excess.shape
    )
    return (corrected_flow_vector, conduct(thermal_profile, spread_wide))


def solution(mesh):
    return jax.shard_map(
        per_device,
        mesh=mesh,
        in_specs=(
            P(None, "wide", "narrow", None),
            P(None, "wide", "narrow", None),
            P("wide", "narrow", None),
            P("wide", "narrow", None),
            P("wide", "narrow", None),
            P(("wide", "narrow"), None),
            P(("wide", "narrow")),
        ),
        out_specs=(P(None, "wide", "narrow", None), P("wide", "narrow", None)),
        check_vma=False,
    )
```

profile of v0, /device:TPU:1, one launch (start us, length us, event | category | flops | bytes accessed | tf_op | source)
XLA Modules:
  0.0 171.2 jit_solution(15021139544594455482)
XLA Ops:
  7.2 0.7 broadcast_multiply_fusion.1
  7.9 0.7 add.74.target
  8.6 1.2 copy-done.2
  9.8 45.6 %flow.1 = (f32[3,16,32,512]{3,2,1,0:T(8,128)}, f32[16,32,512]{2,1,0:T(8,128)S(1)}, f32[4,512,128]{2,1,0:T(8,128)S(1)}) custom-call(f32[3,16,32,512]{3,2,1,0:T(8,128)} %vel_in.1, f32[3,16,32,512]{3,2,1,0:T(8,128)} %push_in.1, f32[16,32,512]{2,1,0:T(8,128)S(1)} %copy-done.2), custom_call_target="tpu_custom_call" | custom-call | tf_op jit(solution)/shard_map/flow/pallas_call | solution.py:301
  55.5 6.4 %slab_heat.1 = f32[8192,128]{1,0:T(8,128)S(1)} custom-call(s32[2048]{0:T(1024)S(1)} %add.74.target, f32[4,512,128]{2,1,0:T(8,128)S(1)} %get-tuple-element.11.heat), custom_call_target="tpu_custom_call" | custom-call | tf_op jit(solution)/shard_map/slab_heat/pallas_call | solution.py:343
  62.0 2.0 %copy-done = f32[8192,128]{1,0:T(8,128)} copy-done((f32[8192,128]{1,0:T(8,128)}, f32[8192,128]{1,0:T(8,128)S(1)}, u32[]{:S(2)}) %copy-start) | copy-done | bytes 4194328
  64.0 1.0 fusion.19
  65.0 1.4 collective-permute-start.4
  66.4 1.3 collective-permute-start.5
  67.8 1.0 copy-done.7
  68.8 1.0 copy-done.8
  69.9 1.0 copy-done.9
  70.9 1.1 copy-done.10
  72.0 0.9 copy-done.14
  72.9 0.9 copy-done.15
  73.8 0.8 copy-done.16
  74.5 56.7 %pressure.1 = (f32[18,32,512]{2,1,0:T(8,128)S(1)}, f32[2,16,512]{2,1,0:T(8,128)S(1)}) custom-call(f32[8,2,32,512]{3,2,1,0:T(8,128)S(1)} %bitcast.6, bf16[512,512]{1,0:T(8,128)(2,1)S(1)} %copy-done.3, bf16[512,512]{1,0:T(8,128)(2,1)S(1)} %copy-done.4, bf16[512,512]{1,0:T(8,128)(2,1)S(1)} %copy-done.5, bf16[512,512]{1,0:T(8,128)(2,1)S(1)} %copy-done.6, ...), custom_call_target="tpu_custom_call" | custom-call | tf_op jit(solution)/shard_map/pressure/pallas_call | solution.py:693
  131.3 3.9 %projection.1 = f32[3,16,32,512]{3,2,1,0:T(8,128)} custom-call(f32[18,32,512]{2,1,0:T(8,128)S(1)} %get-tuple-element.8.press, f32[2,16,512]{2,1,0:T(8,128)S(1)} %get-tuple-element.9.y_halo, f32[3,16,32,512]{3,2,1,0:T(8,128)S(1)} %copy-done.1), custom_call_target="tpu_custom_call" | custom-call | tf_op jit(solution)/shard_map/projection/pallas_call | solution.py:761
  135.2 6.2 %reduce-scatter.4.cloned.1.call-done = f32[1,512,128]{2,1,0:T(8,128)} async-done(((f32[16,512,128]{2,1,0:T(8,128)}), f32[1,512,128]{2,1,0:T(8,128)}) %reduce-scatter.4.cloned.1.call-update) | async-done | bytes 262160
  141.5 1.0 broadcast_multiply_fusion
  142.5 1.3 collective-permute-start.1
  143.8 4.0 %collective-permute-start = (f32[3,32,128]{2,1,0:T(8,128)S(1)}, f32[3,32,128]{2,1,0:T(8,128)S(1)}, u32[]{:S(2)}, u32[]{:S(2)}) collective-permute-start(f32[3,32,128]{2,1,0:T(8,128)S(1)} %get-tuple-element.24), channel_id=1, source_target_pairs={{0,8},{8,16},{16,24},{24,32},{32,40},{40,48},{48,56},{56,64},{64,7... | collective-permute-start | bytes 147464 | tf_op jit(solution)/shard_map/ppermute | solution.py:33
  147.8 4.8 %collective-permute-start.7 = (f32[22,3,128]{2,1,0:T(4,128)S(1)}, f32[22,3,128]{2,1,0:T(4,128)S(1)}, u32[]{:S(2)}, u32[]{:S(2)}) collective-permute-start(f32[22,3,128]{2,1,0:T(4,128)S(1)} %get-tuple-element.19), channel_id=1, source_target_pairs={{1,0},{2,1},{3,2},{4,3},{5,4},{6,5},{7,6},{9,8},{10,9},{11,10},{12... | collective-permute-start | bytes 101384 | tf_op jit(solution)/shard_map/ppermute | solution.py:33
  152.6 3.0 %collective-permute-start.6 = (f32[22,3,128]{2,1,0:T(4,128)S(1)}, f32[22,3,128]{2,1,0:T(4,128)S(1)}, u32[]{:S(2)}, u32[]{:S(2)}) collective-permute-start(f32[22,3,128]{2,1,0:T(4,128)S(1)} %get-tuple-element.18), channel_id=1, source_target_pairs={{0,1},{1,2},{2,3},{3,4},{4,5},{5,6},{6,7},{8,9},{9,10},{10,11},{11... | collective-permute-start | bytes 101384 | tf_op jit(solution)/shard_map/ppermute | solution.py:33
  155.6 1.9 %collective-permute-start.3 = (f32[22,3,128]{2,1,0:T(4,128)S(1)}, f32[22,3,128]{2,1,0:T(4,128)S(1)}, u32[]{:S(2)}, u32[]{:S(2)}) collective-permute-start(f32[22,3,128]{2,1,0:T(4,128)S(1)} %get-tuple-element.21), channel_id=1, source_target_pairs={{1,0},{2,1},{3,2},{4,3},{5,4},{6,5},{7,6},{9,8},{10,9},{11,10},{12... | collective-permute-start | bytes 101384 | tf_op jit(solution)/shard_map/ppermute | solution.py:33
  157.6 3.6 %collective-permute-start.2 = (f32[22,3,128]{2,1,0:T(4,128)S(1)}, f32[22,3,128]{2,1,0:T(4,128)S(1)}, u32[]{:S(2)}, u32[]{:S(2)}) collective-permute-start(f32[22,3,128]{2,1,0:T(4,128)S(1)} %get-tuple-element.20), channel_id=1, source_target_pairs={{0,1},{1,2},{2,3},{3,4},{4,5},{5,6},{6,7},{8,9},{9,10},{10,11},{11... | collective-permute-start | bytes 101384 | tf_op jit(solution)/shard_map/ppermute | solution.py:33
  161.3 1.0 collective-permute-done.2
  162.4 0.2 fusion.15
  162.6 0.3 fusion.4
  162.9 0.2 fusion.16
  163.0 0.3 fusion.9
  163.4 0.9 fusion.14
  (48 shorter events, 0.5 us)
Async XLA Ops:
  7.2 134.3 %reduce-scatter.4.cloned.1.call-start = ((), (), s32[]{:S(2)}) async-start(), calls=%async_computation.1 | async-start | bytes 4456448
  8.6 1.2 copy-start.2
  61.9 2.0 %copy-start = (f32[8192,128]{1,0:T(8,128)}, f32[8192,128]{1,0:T(8,128)S(1)}, u32[]{:S(2)}) copy-start(f32[8192,128]{1,0:T(8,128)S(1)} %slab_heat.1) | copy-start | bytes 12582916
  63.9 3.8 %copy-start.3 = (bf16[512,512]{1,0:T(8,128)(2,1)S(1)}, bf16[512,512]{1,0:T(8,128)(2,1)}, u32[]{:S(2)}) copy-start(bf16[512,512]{1,0:T(8,128)(2,1)} %constant.17.clone.fe_h) | copy-start | bytes 1572868
  63.9 3.8 %copy-start.4 = (bf16[512,512]{1,0:T(8,128)(2,1)S(1)}, bf16[512,512]{1,0:T(8,128)(2,1)}, u32[]{:S(2)}) copy-start(bf16[512,512]{1,0:T(8,128)(2,1)} %constant.40.clone.fe_l) | copy-start | bytes 1572868
  63.9 3.8 %copy-start.5 = (bf16[512,512]{1,0:T(8,128)(2,1)S(1)}, bf16[512,512]{1,0:T(8,128)(2,1)}, u32[]{:S(2)}) copy-start(bf16[512,512]{1,0:T(8,128)(2,1)} %constant.41.clone.fo_h) | copy-start | bytes 1572868
  63.9 3.8 %copy-start.6 = (bf16[512,512]{1,0:T(8,128)(2,1)S(1)}, bf16[512,512]{1,0:T(8,128)(2,1)}, u32[]{:S(2)}) copy-start(bf16[512,512]{1,0:T(8,128)(2,1)} %constant.42.clone.fo_l) | copy-start | bytes 1572868
  63.9 3.8 %copy-start.11 = (bf16[256,256]{1,0:T(8,128)(2,1)S(1)}, bf16[256,256]{1,0:T(8,128)(2,1)}, u32[]{:S(2)}) copy-start(bf16[256,256]{1,0:T(8,128)(2,1)} %constant.47.clone.cy_h) | copy-start | bytes 393220
  63.9 3.8 %copy-start.12 = (bf16[256,256]{1,0:T(8,128)(2,1)S(1)}, bf16[256,256]{1,0:T(8,128)(2,1)}, u32[]{:S(2)}) copy-start(bf16[256,256]{1,0:T(8,128)(2,1)} %constant.48.clone.cy_l) | copy-start | bytes 393220
  63.9 3.8 %copy-start.13 = (bf16[256,256]{1,0:T(8,128)(2,1)S(1)}, bf16[256,256]{1,0:T(8,128)(2,1)}, u32[]{:S(2)}) copy-start(bf16[256,256]{1,0:T(8,128)(2,1)} %constant.49.clone.iy_h) | copy-start | bytes 393220
  64.0 67.3 %copy-start.1 = (f32[3,16,32,512]{3,2,1,0:T(8,128)S(1)}, f32[3,16,32,512]{3,2,1,0:T(8,128)}, u32[]{:S(2)}) copy-start(f32[3,16,32,512]{3,2,1,0:T(8,128)} %get-tuple-element.10.current) | copy-start | bytes 9437188
  65.0 70.2 %collective-permute-start.4 = (f32[3,32,128]{2,1,0:T(8,128)S(1)}, f32[3,32,128]{2,1,0:T(8,128)S(1)}, u32[]{:S(2)}, u32[]{:S(2)}) collective-permute-start(f32[3,32,128]{2,1,0:T(8,128)S(1)} %get-tuple-element.23), channel_id=1, source_target_pairs={{0,8},{8,16},{16,24},{24,32},{32,40},{40,48},{48,56},{56,64},{64,7... | collective-permute-start | bytes 147464 | tf_op jit(solution)/shard_map/ppermute | solution.py:33
  66.4 68.8 %collective-permute-start.5 = (f32[3,32,128]{2,1,0:T(8,128)S(1)}, f32[3,32,128]{2,1,0:T(8,128)S(1)}, u32[]{:S(2)}, u32[]{:S(2)}) collective-permute-start(f32[3,32,128]{2,1,0:T(8,128)S(1)} %get-tuple-element.22), channel_id=1, source_target_pairs={{8,0},{16,8},{24,16},{32,24},{40,32},{48,40},{56,48},{64,56},{72,6... | collective-permute-start | bytes 147464 | tf_op jit(solution)/shard_map/ppermute | solution.py:33
  67.8 1.0 copy-start.7
  68.8 1.0 copy-start.8
  69.9 1.0 copy-start.9
  70.9 1.1 copy-start.10
  72.0 0.9 copy-start.14
  72.9 0.9 copy-start.15
  73.8 0.8 copy-start.16
  131.3 3.9 %copy-start.17 = (f32[16,32,128]{2,1,0:T(8,128)S(1)}, f32[16,32,128]{2,1,0:T(8,128)}, u32[]{:S(2)}) copy-start(f32[16,32,128]{2,1,0:T(8,128)} %param.25) | copy-start | bytes 786436
  131.3 11.2 %copy-start.18 = (f32[16,32,128]{2,1,0:T(8,128)S(1)}, f32[16,32,128]{2,1,0:T(8,128)}, u32[]{:S(2)}) copy-start(f32[16,32,128]{2,1,0:T(8,128)} %param.24) | copy-start | bytes 786436
  142.5 13.1 %collective-permute-start.1 = (f32[3,32,128]{2,1,0:T(8,128)S(1)}, f32[3,32,128]{2,1,0:T(8,128)S(1)}, u32[]{:S(2)}, u32[]{:S(2)}) collective-permute-start(f32[3,32,128]{2,1,0:T(8,128)S(1)} %get-tuple-element.25), channel_id=1, source_target_pairs={{8,0},{16,8},{24,16},{32,24},{40,32},{48,40},{56,48},{64,56},{72,6... | collective-permute-start | bytes 147464 | tf_op jit(solution)/shard_map/ppermute | solution.py:33
  143.8 11.8 %collective-permute-start = (f32[3,32,128]{2,1,0:T(8,128)S(1)}, f32[3,32,128]{2,1,0:T(8,128)S(1)}, u32[]{:S(2)}, u32[]{:S(2)}) collective-permute-start(f32[3,32,128]{2,1,0:T(8,128)S(1)} %get-tuple-element.24), channel_id=1, source_target_pairs={{0,8},{8,16},{16,24},{24,32},{32,40},{40,48},{48,56},{56,64},{64,7... | collective-permute-start | bytes 147464 | tf_op jit(solution)/shard_map/ppermute | solution.py:33
  147.8 13.4 %collective-permute-start.7 = (f32[22,3,128]{2,1,0:T(4,128)S(1)}, f32[22,3,128]{2,1,0:T(4,128)S(1)}, u32[]{:S(2)}, u32[]{:S(2)}) collective-permute-start(f32[22,3,128]{2,1,0:T(4,128)S(1)} %get-tuple-element.19), channel_id=1, source_target_pairs={{1,0},{2,1},{3,2},{4,3},{5,4},{6,5},{7,6},{9,8},{10,9},{11,10},{12... | collective-permute-start | bytes 101384 | tf_op jit(solution)/shard_map/ppermute | solution.py:33
  152.6 8.6 %collective-permute-start.6 = (f32[22,3,128]{2,1,0:T(4,128)S(1)}, f32[22,3,128]{2,1,0:T(4,128)S(1)}, u32[]{:S(2)}, u32[]{:S(2)}) collective-permute-start(f32[22,3,128]{2,1,0:T(4,128)S(1)} %get-tuple-element.18), channel_id=1, source_target_pairs={{0,1},{1,2},{2,3},{3,4},{4,5},{5,6},{6,7},{8,9},{9,10},{10,11},{11... | collective-permute-start | bytes 101384 | tf_op jit(solution)/shard_map/ppermute | solution.py:33
  155.6 5.7 %collective-permute-start.3 = (f32[22,3,128]{2,1,0:T(4,128)S(1)}, f32[22,3,128]{2,1,0:T(4,128)S(1)}, u32[]{:S(2)}, u32[]{:S(2)}) collective-permute-start(f32[22,3,128]{2,1,0:T(4,128)S(1)} %get-tuple-element.21), channel_id=1, source_target_pairs={{1,0},{2,1},{3,2},{4,3},{5,4},{6,5},{7,6},{9,8},{10,9},{11,10},{12... | collective-permute-start | bytes 101384 | tf_op jit(solution)/shard_map/ppermute | solution.py:33
  157.6 4.8 %collective-permute-start.2 = (f32[22,3,128]{2,1,0:T(4,128)S(1)}, f32[22,3,128]{2,1,0:T(4,128)S(1)}, u32[]{:S(2)}, u32[]{:S(2)}) collective-permute-start(f32[22,3,128]{2,1,0:T(4,128)S(1)} %get-tuple-element.20), channel_id=1, source_target_pairs={{0,1},{1,2},{2,3},{3,4},{4,5},{5,6},{6,7},{8,9},{9,10},{10,11},{11... | collective-permute-start | bytes 101384 | tf_op jit(solution)/shard_map/ppermute | solution.py:33
Sparse Core Ops, SparseCore 0:
  64.1 77.3 reduce-scatter.3
where the time goes:
time: 173 us; the launch traced here: 171 us
  Pallas kernels  113 us (65%)
  starting transfers between devices  21.3 us (12%)
  between operations  14.4 us (8%)
  local copies, waits for them, and re-layouts  11.5 us (7%)
  waiting for transfers between devices  7.3 us (4%)
  other arithmetic  4.02 us (2%)
    pallas_call x1, Pallas kernels, solve_pressure(): pl.pallas_call(functools.partial(pressure_kernel, n_wide, n_narrow), out_...  56.7 us
    pallas_call x1, Pallas kernels, flow(): pl.pallas_call(functools.partial(flow_kernel, n_wide, n_narrow), out_shap...  45.6 us
    ppermute x8, starting transfers between devices, shifted(): return lax.ppermute(x, axis, pairs)  21.3 us
    unnamed x40, local copies, waits for them, and re-layouts  10 us
    pallas_call x1, Pallas kernels, slab_heat(): pl.pallas_call(gather_kernel, out_shape=jax.ShapeDtypeStruct((lines, 128)...  6.45 us
    unnamed x2, waiting for transfers between devices  6.26 us
    pallas_call x1, Pallas kernels, project(): pl.pallas_call(project_kernel, grid=(x_local // planes,), out_shape=jax.S...  3.86 us
  transfers between devices with their start and end apart: 9, of which 2 were waited for; matrix products, arithmetic and copies ran while one was open for 1% of the time, Pallas kernels for 35%

commit v1 on v0

--- a/solution.py
+++ b/solution.py
@@ -23,25 +23,7 @@
 penalty = 0.001
 dissipation_factor = 0.1
 GROUPS = 2
-
-
-def shifted(x, axis, up, wrap):
-    size = lax.axis_size(axis)
-    pairs = [(i, (i + 1) % size) for i in range(size if wrap else size - 1)]
-    if not up:
-        pairs = [(j, i) for i, j in pairs]
-    return lax.ppermute(x, axis, pairs)
-
-
-def with_halo(x, sides, width, wrap):
-    for axis, dim in sides:
-        length = x.shape[dim]
-        last = lax.slice_in_dim(x, length - width, length, axis=dim)
-        initial = lax.slice_in_dim(x, 0, width, axis=dim)
-        before = shifted(last, axis, True, wrap)
-        after = shifted(initial, axis, False, wrap)
-        x = jnp.concatenate([before, x, after], axis=dim)
-    return x
+DEEP = STEPS
 
 
 PAD = 8
@@ -403,11 +385,28 @@
 
 def pressure_kernel(
     n_wide, n_narrow,
-    div, fe_h, fe_l, fo_h, fo_l, ie_h, ie_l, io_h, io_l, cy_h, cy_l, iy_h, iy_l, s_y, s_z,
-    press, y_halo,
-    zsend, rbuf, ubuf, vsend, zrecv, rtab, mom, mrecv, absend, ab, xrecv, yrecv, ysend,
-    nf_send, nf_recv, nb_send, nb_recv, wf_send, wf_recv, wb_send, wb_recv, h_send, h_recv,
+    div, slab, substrate, spread, *rest,
 ):
+    table_refs, rest = rest[:12], rest[12:]
+    s_y, s_z, press, y_halo, tp, cp = rest[:6]
+    tables, rest = rest[6:18], rest[18:]
+    (
+        zsend, rbuf, ubuf, vsend, zrecv, rtab, mom, mrecv, absend, ab, xrecv, yrecv, ysend,
+        first_in, first_sum, second_in, part_xr,
+        nf_send, nf_recv, nb_send, nb_recv, wf_send, wf_recv, wb_send, wb_recv, h_send, h_recv,
+        f_send, f_recv, q_send, q_recv, p_send, p_recv, table_sem, own_sem,
+    ) = rest
+    fe_h, fe_l, fo_h, fo_l, ie_h, ie_l, io_h, io_l, cy_h, cy_l, iy_h, iy_l = tables
+    loads = [
+        pltpu.make_async_copy(table_refs[i], tables[i], table_sem.at[i]) for i in range(12)
+    ]
+
+    def loaded(*which):
+        for i in which:
+            loads[i].wait()
+
+    for i in (0, 1, 2, 3, 8, 9, 10, 11, 4, 5, 6, 7):
+        loads[i].start()
     w = lax.axis_index("wide")
     n = lax.axis_index("narrow")
     xps, _, rows, n_z = div.shape
@@ -421,6 +420,129 @@
     def along(k):
         return lax.rem(w + k, n_wide)
 
+    side = math.isqrt(n_wide)
+    half = slab.shape[2] // 2
+    own = (w // side, lax.rem(w, side))
+
+    def peer(way, k):
+        to = lax.rem(own[way] + k, side)
+        return (to, to * side + own[1] if way == 0 else own[0] * side + to)
+
+    def first_source(way, to):
+        return slab.at[to, :, pl.ds(0, half)] if way == 0 else slab.at[:, to, pl.ds(half, half)]
+
+    def first_copy(way, k):
+        to, device = peer(way, k)
+        return pltpu.make_async_remote_copy(
+            src_ref=first_source(way, to), dst_ref=first_in.at[way, k],
+            send_sem=f_send.at[way, k], recv_sem=f_recv.at[way, k],
+            device_id=(device, n), device_id_type=MESH,
+        )
+
+    def own_first(way):
+        return pltpu.make_async_copy(
+            first_source(way, own[way]), first_in.at[way, 0], own_sem.at[way]
+        )
+
+    def second_copy(way, k):
+        to, device = peer(1 - way, k)
+        return pltpu.make_async_remote_copy(
+            src_ref=first_sum.at[way, to], dst_ref=second_in.at[way, k],
+            send_sem=q_send.at[way, k], recv_sem=q_recv.at[way, k],
+            device_id=(device, n), device_id_type=MESH,
+        )
+
+    halves = [(way, k) for way in (0, 1) for k in range(1, side)]
+
+    def first_total():
+        for way in (0, 1):
+            own_first(way).wait()
+        for way, k in halves:
+            first_copy(way, k).wait_recv()
+        step = 32
+        per_slab = half // step
+
+        def add(i, c):
+            at = i // per_slab
+            here = pl.ds(pl.multiple_of(lax.rem(i, per_slab) * step, step), step)
+            for way in (0, 1):
+                total = first_in[way, 0, at, here]
+                for k in range(1, side):
+                    total = total + first_in[way, k, at, here]
+                first_sum[way, at, here] = total
+            return c
+
+        lax.fori_loop(0, side * per_slab, add, 0)
+        for way, k in halves:
+            second_copy(way, k).start()
+
+    planes = substrate.shape[0]
+    part_rows = substrate.shape[1]
+    inside = pl.ds(PAD, part_rows)
+    last_w, last_n = n_wide - 1, n_narrow - 1
+    wide_near = (lax.rem(w + last_w, n_wide), lax.rem(w + 1, n_wide))
+    narrow_near = (lax.rem(n + last_n, n_narrow), lax.rem(n + 1, n_narrow))
+
+    def part_x(field, e, side_):
+        start = planes if side_ else DEEP
+        return pltpu.make_async_remote_copy(
+            src_ref=field.at[pl.ds(start, DEEP), inside], dst_ref=part_xr.at[e, 1 - side_],
+            send_sem=p_send.at[e, side_], recv_sem=p_recv.at[e, 1 - side_],
+            device_id=(wide_near[side_], n), device_id_type=MESH,
+        )
+
+    def part_y(field, e, side_):
+        start = part_rows if side_ else PAD
+        land = 0 if side_ else PAD + part_rows
+        return pltpu.make_async_remote_copy(
+            src_ref=field.at[:, pl.ds(start, PAD)], dst_ref=field.at[:, pl.ds(land, PAD)],
+            send_sem=p_send.at[e, 2 + side_], recv_sem=p_recv.at[e, 3 - side_],
+            device_id=(w, narrow_near[side_]), device_id_type=MESH,
+        )
+
+    def part_x_start(field, e):
+        for i in (0, 1):
+            part_x(field, e, i).start()
+
+    def part_x_end(field, e):
+        for i in (0, 1):
+            part_x(field, e, i).wait_recv()
+        field[0:DEEP, PAD:PAD + part_rows] = jnp.where(w == 0, 0.0, part_xr[e, 0])
+        field[planes + DEEP:, PAD:PAD + part_rows] = jnp.where(w == last_w, 0.0, part_xr[e, 1])
+        for i in (0, 1):
+            part_y(field, e, i).start()
+
+    def part_y_end(field, e):
+        for i in (0, 1):
+            part_y(field, e, i).wait_recv()
+
+        @pl.when(n == 0)
+        def _():
+            field[:, 0:PAD] = jnp.zeros_like(field[:, 0:PAD])
+
+        @pl.when(n == last_n)
+        def _():
+            field[:, PAD + part_rows:] = jnp.zeros_like(field[:, PAD + part_rows:])
+
+        for i in (0, 1):
+            part_x(field, e, i).wait_send()
+            part_y(field, e, i).wait_send()
+
+    def part_start():
+        for way, k in halves:
+            second_copy(way, k).wait_recv()
+        per_half = planes // 2
+        for way in (0, 1):
+            mine = own[1 - way]
+            for i in range(per_half):
+                here = slice(i * part_rows, (i + 1) * part_rows)
+                total = first_sum[way, mine, here]
+                for k in range(1, side):
+                    total = total + second_in[way, k, here]
+                x = way * per_half + i
+                tp[DEEP + x, PAD:PAD + part_rows] = substrate[x] + dissipation_factor * total
+        part_x_start(tp, 0)
+
     barrier = pltpu.get_barrier_semaphore()
 
     def greet_n(k, c):
@@ -456,6 +578,9 @@
             device_id=(w, source), device_id_type=MESH,
         )
 
+    for way in (0, 1):
+        own_first(way).start()
+    loaded(0, 1, 2, 3)
     for g in range(GROUPS):
         even = div[g * per:(g + 1) * per, 0].reshape(per * rows, n_z)
         odd = div[g * per:(g + 1) * per, 1].reshape(per * rows, n_z)
@@ -476,6 +601,11 @@
             return c
 
         lax.fori_loop(1, n_narrow, launch, 0)
+        if g == 0:
+            for way, k in halves:
+                first_copy(way, k).start()
+            cp[DEEP:DEEP + planes, PAD:PAD + part_rows] = spread[...]
+            part_x_start(cp, 1)
 
     s = s_y[...] + s_z[n][0:1, :] + penalty
     root = jnp.sqrt(s * (1.0 + s))
@@ -485,6 +615,9 @@
     for g in range(GROUPS):
         span = slice(g * per, (g + 1) * per)
         rbuf[span, pl.ds(pl.multiple_of(n * rows, rows), rows)] = zsend[n, span]
+        if g == 0:
+            part_x_end(cp, 1)
+            loaded(8, 9)
 
         def arrive(k, c):
             forward_arrival(g, k).wait_recv()
@@ -616,6 +749,7 @@
             device_id=(w, source), device_id_type=MESH,
         )
 
+    loaded(10, 11)
     for g in range(GROUPS):
         span = slice(g * per, (g + 1) * per)
         lines = jnp.concatenate([ubuf[xp] for xp in range(g * per, (g + 1) * per)], axis=1)
@@ -626,22 +760,23 @@
         each(n_narrow, lambda k: backward_copy(g, k).start())
         zrecv[n, span] = vsend[n, span]
 
-    wide_to = {0: along(n_wide - 1), 1: along(1)}
-    narrow_to = {0: across(n_narrow - 1), 1: across(1)}
+    first_total()
+    part_y_end(cp, 1)
+    loaded(4, 5, 6, 7)
 
     def x_halo(side):
         source = 2 * xps if side else 1
         return pltpu.make_async_remote_copy(
             src_ref=press.at[source], dst_ref=xrecv.at[1 - side],
             send_sem=h_send.at[side], recv_sem=h_recv.at[1 - side],
-            device_id=(wide_to[side], n), device_id_type=MESH,
+            device_id=(wide_near[side], n), device_id_type=MESH,
         )
 
     def y_halo_copy(side):
         return pltpu.make_async_remote_copy(
             src_ref=ysend.at[side], dst_ref=yrecv.at[1 - side],
             send_sem=h_send.at[2 + side], recv_sem=h_recv.at[3 - side],
-            device_id=(w, narrow_to[side]), device_id_type=MESH,
+            device_id=(w, narrow_near[side]), device_id_type=MESH,
         )
 
     for g in range(GROUPS):
@@ -663,10 +798,15 @@
                 ysend[1, x] = plane[rows - 1]
         if g == 0:
             x_halo(0).start()
+            part_start()
     x_halo(1).start()
     y_halo_copy(0).start()
     y_halo_copy(1).start()
-
+    part_x_end(tp, 0)
+
+    for way, k in halves:
+        first_copy(way, k).wait_send()
+        second_copy(way, k).wait_send()
     for g in range(GROUPS):
         each(n_narrow, lambda k: forward_copy(g, k).wait_send())
         each(n_narrow, lambda k: backward_copy(g, k).wait_send())
@@ -678,9 +818,10 @@
     press[0] = xrecv[0]
     press[2 * xps + 1] = xrecv[1]
     y_halo[...] = yrecv[...]
-
-
-def solve_pressure(divergence):
+    part_y_end(tp, 0)
+
+
+def solve_pressure(divergence, slab, substrate, spread):
     n_wide, n_narrow = lax.axis_size("wide"), lax.axis_size("narrow")
     x_local, rows, n_z = divergence.shape
     n_y = rows * n_narrow
@@ -690,15 +831,23 @@
     field = (xps, n_y, 128)
     turned = (n_narrow, xps, rows, 128)
     chunk_rows = n_y // n_wide
+    side = math.isqrt(n_wide)
+    planes, part_rows, depth = substrate.shape
+    half = planes * part_rows // 2
+    part = (planes + 2 * DEEP, part_rows + 2 * PAD, depth)
+    any_space = pl.BlockSpec(memory_space=pl.ANY)
     return pl.pallas_call(
         functools.partial(pressure_kernel, n_wide, n_narrow),
         out_shape=[
             jax.ShapeDtypeStruct((x_local + 2, rows, n_z), F32),
             jax.ShapeDtypeStruct((2, x_local, n_z), F32),
+            jax.ShapeDtypeStruct(part, F32),
+            jax.ShapeDtypeStruct(part, F32),
         ],
-        in_specs=[VM] * (1 + len(tables)),
-        out_specs=[VM, VM],
-        scratch_shapes=[
+        in_specs=[VM, any_space, VM, VM] + [any_space] * 12 + [VM, VM],
+        out_specs=[VM] * 4,
+        scratch_shapes=[pltpu.VMEM(t.shape, BF16) for t in tables[:12]]
+        + [
             pltpu.VMEM(turned, F32),
             pltpu.VMEM(field, F32),
             pltpu.VMEM(field, F32),
@@ -712,6 +861,10 @@
             pltpu.VMEM((2, rows, n_z), F32),
             pltpu.VMEM((2, x_local, n_z), F32),
             pltpu.VMEM((2, x_local, n_z), F32),
+            pltpu.VMEM((2, side, side, half, depth), F32),
+            pltpu.VMEM((2, side, half, depth), F32),
+            pltpu.VMEM((2, side, half, depth), F32),
+            pltpu.VMEM((2, 2, DEEP, part_rows, depth), F32),
             dma((GROUPS, n_narrow)),
             dma((GROUPS, n_narrow)),
             dma((GROUPS, n_narrow)),
@@ -722,12 +875,44 @@
             dma((n_wide,)),
             dma((4,)),
             dma((4,)),
+            dma((2, side)),
+            dma((2, side)),
+            dma((2, side)),
+            dma((2, side)),
+            dma((2, 4)),
+            dma((2, 4)),
+            dma((12,)),
+            dma((2,)),
         ],
         compiler_params=pltpu.CompilerParams(
-            collective_id=1, has_side_effects=True, vmem_limit_bytes=40 * 2**20
+            collective_id=1, has_side_effects=True, vmem_limit_bytes=52 * 2**20
         ),
         name="pressure",
-    )(divergence.reshape(xps, 2, rows, n_z), *tables)
+    )(
+        divergence.reshape(xps, 2, rows, n_z),
+        slab.reshape(side, side, 2 * half, depth),
+        substrate, spread, *tables,
+    )
+
+
+def conduct(step, source, coefficient, target):
+    planes, rows, depth = coefficient.shape
+    lane = lax.broadcasted_iota(jnp.int32, (rows, depth), 1)
+
+    def plane(x, below):
+        p = source[x]
+        above = source[x + 1]
+        around = above + below + pltpu.roll(p, 1, 0) + pltpu.roll(p, rows - 1, 0)
+        around += jnp.where(lane == 0, 0.0, pltpu.roll(p, 1, 1))
+        around += jnp.where(lane == depth - 1, 0.0, pltpu.roll(p, depth - 1, 1))
+        new = p + coefficient[x] * (around - 6.0 * p)
+        if step == STEPS - 1:
+            target[x - DEEP] = new[PAD:rows - PAD]
+        else:
+            target[x] = new
+        return p
+
+    lax.fori_loop(step + 1, planes - step - 1, plane, source[step])
 
 
 def y_step(plane, before, after, ahead):
@@ -738,9 +923,15 @@
     return jnp.where(row == 0, before, pltpu.roll(plane, 1, 0))
 
 
-def project_kernel(press, y_halo, current, out):
+def project_kernel(press, y_halo, tp, cp, current, out, part, tq):
     step = pl.program_id(0)
     n_z = press.shape[2]
+    for i in range(STEPS):
+
+        @pl.when(step == i)
+        def _():
+            conduct(i, (tp, tq, tq)[i], cp, (tq, tq, part)[i])
+
     for i in range(current.shape[1]):
         x = step * current.shape[1] + i
         p = press[x + 1]
@@ -753,34 +944,21 @@
         out[2, i] = current[2, i] - 0.5 * (pltpu.roll(p, n_z - 1, 1) - pltpu.roll(p, 1, 1))
 
 
-def project(current, divergence):
-    press, y_halo = solve_pressure(divergence)
+def project(current, press, y_halo, tp, cp):
     _, x_local, rows, n_z = current.shape
     planes = 2
     spec = pl.BlockSpec((3, planes, rows, n_z), lambda i: (0, i, 0, 0))
+    part = (tp.shape[0] - 2 * DEEP, tp.shape[1] - 2 * PAD, tp.shape[2])
     return pl.pallas_call(
         project_kernel,
         grid=(x_local // planes,),
-        out_shape=jax.ShapeDtypeStruct(current.shape, F32),
-        in_specs=[VM, VM, spec],
-        out_specs=spec,
+        out_shape=[jax.ShapeDtypeStruct(current.shape, F32), jax.ShapeDtypeStruct(part, F32)],
+        in_specs=[VM, VM, VM, VM, spec],
+        out_specs=[spec, pl.BlockSpec(part, lambda i: (0, 0, 0))],
+        scratch_shapes=[pltpu.VMEM(tp.shape, F32)],
         compiler_params=pltpu.CompilerParams(vmem_limit_bytes=20 * 2**20),
         name="projection",
-    )(press, y_halo, current)
-
-
-def conduct(thermal_profile, spread_wide):
-    sides = (("wide", 0), ("narrow", 1))
-    t = with_halo(thermal_profile, sides, STEPS, False)
-    coefficient = spread_wide
-    for _ in range(STEPS):
-        center = t[1:-1, 1:-1]
-        coefficient = coefficient[1:-1, 1:-1]
-        around = t[2:, 1:-1] + t[:-2, 1:-1] + t[1:-1, 2:] + t[1:-1, :-2]
-        ahead = jnp.pad(center[:, :, 1:], ((0, 0), (0, 0), (0, 1)))
-        behind = jnp.pad(center[:, :, :-1], ((0, 0), (0, 0), (1, 0)))
-        t = center + coefficient * (around + ahead + behind - 6.0 * center)
-    return t
+    )(press, y_halo, tp, cp, current)
 
 
 def per_device(
@@ -793,23 +971,15 @@
     source_part_line,
 ):
     current, divergence, heat = flow(material_flow_vector, tool_push_density, tool_warmth_excess)
-    corrected_flow_vector = project(current, divergence)
-    spread_wide = with_halo(spread_coefficient, (("wide", 0), ("narrow", 1)), STEPS, False)
     slab_ids = source_owner_sheet[:, 0]
     slab_count = lax.axis_size("wide")
     component_lines = substrate_warmth_excess.shape[0] * substrate_warmth_excess.shape[1]
     target = slab_ids * component_lines + source_part_line
     partial_value = slab_heat(target, heat, slab_count * component_lines)
-    substrate_energy_input = lax.psum_scatter(
-        partial_value.reshape(slab_count, component_lines, 128),
-        "wide",
-        scatter_dimension=0,
-        tiled=True,
+    solved = solve_pressure(
+        divergence, partial_value, substrate_warmth_excess, spread_coefficient
     )
-    thermal_profile = substrate_warmth_excess + dissipation_factor * substrate_energy_input.reshape(
-        substrate_warmth_excess.shape
-    )
-    return (corrected_flow_vector, conduct(thermal_profile, spread_wide))
+    return tuple(project(current, *solved))
 
 
 def solution(mesh):

time: 173 us -> 136 us (0.79)
  starting transfers between devices: 21.3 us -> 0 us
  between operations: 14.4 us -> 0.81 us
  Pallas kernels: 113 us -> 126 us
  waiting for transfers between devices: 7.3 us -> 0 us
  local copies, waits for them, and re-layouts: 11.5 us -> 6.61 us
  other arithmetic: 4.02 us -> 1.4 us
    ppermute x8 -> x0, starting transfers between devices: 21.3 us -> none  [shifted(): return lax.ppermute(x, axis, pairs)]
    pallas_call x1, Pallas kernels: 56.7 us -> 66.2 us  [solve_pressure(): pl.pallas_call(functools.partial(pressure_kernel, n_wide, n_narrow), out_...]
    unnamed x2 -> x0, waiting for transfers between devices: 6.26 us -> none
    pallas_call x1, Pallas kernels: 3.86 us -> 7.98 us  [project(): pl.pallas_call(project_kernel, grid=(x_local // planes,), out_shape=[jax....]
    unnamed x40 -> x32, local copies, waits for them, and re-layouts: 10 us -> 6.61 us
  transfers between devices with their start and end apart: 9 -> 0, of which waited for: 2 -> 0; matrix products, arithmetic and copies ran while one was open for 1% -> 0% of each run, Pallas kernels for 35% -> 0%
where the time goes in v1:
time: 136 us; the launch traced here: 135 us
  Pallas kernels  126 us (93%)
  local copies, waits for them, and re-layouts  6.61 us (5%)
  other arithmetic  1.4 us (1%)
    pallas_call x1, Pallas kernels, solve_pressure(): pl.pallas_call(functools.partial(pressure_kernel, n_wide, n_narrow), out_...  66.2 us
    pallas_call x1, Pallas kernels, flow(): pl.pallas_call(functools.partial(flow_kernel, n_wide, n_narrow), out_shap...  45.7 us
    pallas_call x1, Pallas kernels, project(): pl.pallas_call(project_kernel, grid=(x_local // planes,), out_shape=[jax....  7.98 us
    unnamed x32, local copies, waits for them, and re-layouts  6.61 us
    pallas_call x1, Pallas kernels, slab_heat(): pl.pallas_call(gather_kernel, out_shape=jax.ShapeDtypeStruct((lines, 128)...  6.5 us

profile of v1, /device:TPU:1, one launch (start us, length us, event | category | flops | bytes accessed | tf_op | source)
XLA Modules:
  0.0 135.2 jit_solution(6285421106865035097)
XLA Ops:
  0.6 0.7 broadcast_multiply_fusion
  1.3 0.7 add.3.target
  2.0 1.2 copy-done.3
  3.3 45.7 %flow.1 = (f32[3,16,32,512]{3,2,1,0:T(8,128)}, f32[16,32,512]{2,1,0:T(8,128)S(1)}, f32[4,512,128]{2,1,0:T(8,128)S(1)}) custom-call(f32[3,16,32,512]{3,2,1,0:T(8,128)} %vel_in.1, f32[3,16,32,512]{3,2,1,0:T(8,128)} %push_in.1, f32[16,32,512]{2,1,0:T(8,128)S(1)} %copy-done.3), custom_call_target="tpu_custom_call" | custom-call | tf_op jit(solution)/shard_map/flow/pallas_call | solution.py:283
  49.0 0.0 copy-start.4
  49.0 0.0 copy-start.7
  49.0 0.0 copy-start.8
  49.0 0.0 copy-start.9
  49.0 0.0 copy-start.10
  49.0 0.0 copy-start.11
  49.0 0.0 copy-start.12
  49.0 0.0 copy-start.13
  49.0 0.0 copy-start.14
  49.1 0.0 copy-start.15
  49.1 6.5 %slab_heat.1 = f32[8192,128]{1,0:T(8,128)S(1)} custom-call(s32[2048]{0:T(1024)S(1)} %add.3.target, f32[4,512,128]{2,1,0:T(8,128)S(1)} %get-tuple-element.10.heat), custom_call_target="tpu_custom_call" | custom-call | tf_op jit(solution)/shard_map/slab_heat/pallas_call | solution.py:325
  55.6 0.0 copy-done.4
  55.6 0.0 copy-start
  55.6 2.0 %copy-done = f32[8192,128]{1,0:T(8,128)} copy-done((f32[8192,128]{1,0:T(8,128)}, f32[8192,128]{1,0:T(8,128)S(1)}, u32[]{:S(2)}) %copy-start) | copy-done | bytes 4194328
  57.5 0.0 copy-done.7
  57.6 0.0 copy-done.8
  57.6 0.0 copy-done.9
  57.6 0.0 copy-done.10
  57.6 0.0 copy-done.11
  57.6 0.0 copy-done.12
  57.6 0.0 copy-done.13
  57.6 0.0 copy-done.14
  57.6 0.0 copy-done.15
  57.6 66.2 %pressure.1 = (f32[18,32,512]{2,1,0:T(8,128)}, f32[2,16,512]{2,1,0:T(8,128)S(1)}, f32[22,48,128]{2,1,0:T(8,128)}, f32[22,48,128]{2,1,0:T(8,128)}) custom-call(f32[8,2,32,512]{3,2,1,0:T(8,128)} %bitcast.4, f32[4,4,512,128]{3,2,1,0:T(8,128)} %bitcast.3, f32[16,32,128]{2,1,0:T(8,128)S(1)} %copy-done.8, f32[16,32,128]{2,1,0:T(8,128)S(1)} %copy-done.9, ...), custom_call_target="tpu_custom_call" | custom-call | tf_op jit(solution)/shard_map/pressure/pallas_call | solution.py:839
  123.8 1.3 copy-done.2
  125.1 1.0 copy-done.5
  126.1 1.0 copy-done.6
  127.2 8.0 %projection.1 = (f32[3,16,32,512]{3,2,1,0:T(8,128)}, f32[16,32,128]{2,1,0:T(8,128)}) custom-call(f32[18,32,512]{2,1,0:T(8,128)S(1)} %copy-done.2, f32[2,16,512]{2,1,0:T(8,128)S(1)} %get-tuple-element.12.y_halo, f32[22,48,128]{2,1,0:T(8,128)S(1)} %copy-done.5, f32[22,48,128]{2,1,0:T(8,128)S(1)} %copy-done.6, f32[3,16,32,512]{3,2,1,0:T(8,128)S(1)} %copy-done.1), custom_call_target="tpu_custom_call" | custom-call | tf_op jit(solution)/shard_map/projection/pallas_call | solution.py:952
  (6 shorter events, 0.0 us)
Async XLA Ops:
  2.0 1.2 copy-start.3
  49.0 6.6 %copy-start.4 = (f32[16,32,512]{2,1,0:T(8,128)}, f32[16,32,512]{2,1,0:T(8,128)S(1)}, u32[]{:S(2)}) copy-start(f32[16,32,512]{2,1,0:T(8,128)S(1)} %get-tuple-element.9) | copy-start | bytes 3145732
  49.0 8.6 %copy-start.7 = (bf16[512,512]{1,0:T(8,128)(2,1)S(1)}, bf16[512,512]{1,0:T(8,128)(2,1)}, u32[]{:S(2)}) copy-start(bf16[512,512]{1,0:T(8,128)(2,1)} %constant.30.clone.rest_0_) | copy-start | bytes 1572868
  49.0 8.6 %copy-start.8 = (f32[16,32,128]{2,1,0:T(8,128)S(1)}, f32[16,32,128]{2,1,0:T(8,128)}, u32[]{:S(2)}) copy-start(f32[16,32,128]{2,1,0:T(8,128)} %substrate.1) | copy-start | bytes 786436
  49.0 8.6 %copy-start.9 = (f32[16,32,128]{2,1,0:T(8,128)S(1)}, f32[16,32,128]{2,1,0:T(8,128)}, u32[]{:S(2)}) copy-start(f32[16,32,128]{2,1,0:T(8,128)} %spread.1) | copy-start | bytes 786436
  49.0 8.6 %copy-start.10 = (f32[256,128]{1,0:T(8,128)S(1)}, f32[256,128]{1,0:T(8,128)}, u32[]{:S(2)}) copy-start(f32[256,128]{1,0:T(8,128)} %constant.42.clone.rest_12_) | copy-start | bytes 393220
  49.0 8.6 %copy-start.11 = (bf16[256,256]{1,0:T(8,128)(2,1)S(1)}, bf16[256,256]{1,0:T(8,128)(2,1)}, u32[]{:S(2)}) copy-start(bf16[256,256]{1,0:T(8,128)(2,1)} %constant.41.clone.rest_11_) | copy-start | bytes 393220
  49.0 8.5 %copy-start.12 = (bf16[256,256]{1,0:T(8,128)(2,1)S(1)}, bf16[256,256]{1,0:T(8,128)(2,1)}, u32[]{:S(2)}) copy-start(bf16[256,256]{1,0:T(8,128)(2,1)} %constant.40.clone.rest_10_) | copy-start | bytes 393220
  49.0 8.5 %copy-start.13 = (bf16[256,256]{1,0:T(8,128)(2,1)S(1)}, bf16[256,256]{1,0:T(8,128)(2,1)}, u32[]{:S(2)}) copy-start(bf16[256,256]{1,0:T(8,128)(2,1)} %constant.39.clone.rest_9_) | copy-start | bytes 393220
  49.0 8.5 %copy-start.14 = (bf16[256,256]{1,0:T(8,128)(2,1)S(1)}, bf16[256,256]{1,0:T(8,128)(2,1)}, u32[]{:S(2)}) copy-start(bf16[256,256]{1,0:T(8,128)(2,1)} %constant.38.clone.rest_8_) | copy-start | bytes 393220
  49.1 8.5 %copy-start.15 = (f32[8,8,128]{2,1,0:T(8,128)S(1)}, f32[8,8,128]{2,1,0:T(8,128)}, u32[]{:S(2)}) copy-start(f32[8,8,128]{2,1,0:T(8,128)} %constant.43.clone.rest_13_) | copy-start | bytes 98308
  55.6 2.0 %copy-start = (f32[8192,128]{1,0:T(8,128)}, f32[8192,128]{1,0:T(8,128)S(1)}, u32[]{:S(2)}) copy-start(f32[8192,128]{1,0:T(8,128)S(1)} %slab_heat.1) | copy-start | bytes 12582916
  57.6 66.2 %copy-start.1 = (f32[3,16,32,512]{3,2,1,0:T(8,128)S(1)}, f32[3,16,32,512]{3,2,1,0:T(8,128)}, u32[]{:S(2)}) copy-start(f32[3,16,32,512]{3,2,1,0:T(8,128)} %get-tuple-element.15.current) | copy-start | bytes 9437188
  123.8 1.3 copy-start.2
  125.1 1.0 copy-start.5
  126.1 1.0 copy-start.6

commit v2 on v1

--- a/solution.py
+++ b/solution.py
@@ -53,8 +53,7 @@
 
     loads = [
         pltpu.make_async_copy(vel_in, velp.at[:, pl.ds(1, planes), body], load_sem.at[0]),
-        pltpu.make_async_copy(warmth_in, lz, load_sem.at[1]),
-        pltpu.make_async_copy(push_in, push, load_sem.at[2]),
+        pltpu.make_async_copy(push_in, push, load_sem.at[1]),
     ]
     for load in loads:
         load.start()
@@ -122,13 +121,12 @@
     vel_y = y_pair(0, vel_ys, vel_yr)
     for copy in vel_x + vel_y:
         copy.start()
+
+    def zener_log(x):
+        lz[x] = (zener_energy / stress_exponent) * (1.0 / warmth_in[x] - 1.0)
+
+    all_x(zener_log)
     loads[1].wait()
-
-    def zener_log(x):
-        lz[x] = (zener_energy / stress_exponent) * (1.0 / lz[x] - 1.0)
-
-    all_x(zener_log)
-    loads[2].wait()
 
     def excess(src, x, r):
         here = slice(PAD + STRIP * r, PAD + STRIP * (r + 1))
@@ -143,8 +141,8 @@
         return 0.5 * diagonal + 0.25 * (xy * xy + xz * xz + yz * yz)
 
     def mu_plane(src, mup, ys, with_heat):
-        def plane(x):
-            for r in range(strips):
+        def plane(x, which):
+            for r in which:
                 part = slice(STRIP * r, STRIP * (r + 1))
                 extra = excess(src, x, r)
                 rate_sq = extra + rate_base**2
@@ -164,8 +162,8 @@
         return plane
 
     def advance_plane(mup, final):
-        def plane(x):
-            for r in range(strips):
+        def plane(x, which):
+            for r in which:
                 part = slice(STRIP * r, STRIP * (r + 1))
                 here = slice(PAD + STRIP * r, PAD + STRIP * (r + 1))
                 up = slice(PAD + STRIP * r + 1, PAD + STRIP * (r + 1) + 1)
@@ -199,14 +197,17 @@
 
         return plane
 
-    def stage(action, arriving_x, arriving_y, fill):
+    def stage(action, arriving_x, arriving_y, fill, fill_x=None):
+        all_x(lambda x: action(x, range(1, strips - 1)), 1, planes - 1)
         for copy in arriving_y:
             copy.wait_recv()
         fill()
-        all_x(action, 1, planes - 1)
+        all_x(lambda x: action(x, (0, strips - 1)), 1, planes - 1)
         for copy in arriving_x:
             copy.wait_recv()
-        all_x(lambda i: action(i * (planes - 1)), 0, 2)
+        if fill_x is not None:
+            fill_x()
+        all_x(lambda i: action(i * (planes - 1), range(strips)), 0, 2)
 
     stage(mu_plane(velp, mup0, mu_ys0, False), vel_x, vel_y,
           lambda: y_fill(velp, vel_yr, (0, 1, 2)))
@@ -246,8 +247,8 @@
 
         all_x(fill)
 
-    def div_plane(x):
-        for r in range(strips):
+    def div_plane(x, which):
+        for r in which:
             part = slice(STRIP * r, STRIP * (r + 1))
             here = slice(PAD + STRIP * r, PAD + STRIP * (r + 1))
             up = slice(PAD + STRIP * r + 1, PAD + STRIP * (r + 1) + 1)
@@ -257,15 +258,11 @@
             total += provp[1, x + 1, up] - provp[1, x + 1, down]
             div[x, part] = 0.5 * (total + (z_ahead(u) - z_behind(u)))
 
-    for copy in mom_y:
-        copy.wait_recv()
-    fill_rows()
-    all_x(div_plane, 1, planes - 1)
-    for copy in mom_x:
-        copy.wait_recv()
-    provp[0, 0, body] = mom_xr[0]
-    provp[0, planes + 1, body] = mom_xr[1]
-    all_x(lambda i: div_plane(i * (planes - 1)), 0, 2)
+    def fill_planes():
+        provp[0, 0, body] = mom_xr[0]
+        provp[0, planes + 1, body] = mom_xr[1]
+
+    stage(div_plane, mom_x, mom_y, fill_rows, fill_planes)
     for copy in mom_x + mom_y:
         copy.wait_send()
 
@@ -287,10 +284,10 @@
             jax.ShapeDtypeStruct((planes, rows, n_z), F32),
             jax.ShapeDtypeStruct((n_z // 128, planes * rows, 128), F32),
         ],
-        in_specs=[any_space] * 3,
+        in_specs=[any_space, any_space, VM],
         out_specs=[VM] * 3,
         scratch_shapes=[pltpu.VMEM(shape, F32) for shape in shapes]
-        + [dma((3,)), dma((5, 4)), dma((5, 4))],
+        + [dma((2,)), dma((5, 4)), dma((5, 4))],
         compiler_params=pltpu.CompilerParams(
             collective_id=2, has_side_effects=True, vmem_limit_bytes=48 * 2**20
         ),
@@ -357,9 +354,8 @@
     basis_z, symbol_z = real_basis(n_z)
     basis_y, symbol_y = real_basis(n_y)
     forward = basis_z.T
-    swapped = forward.reshape(n_z, n_z // 128, 2, 64)[:, :, ::-1].reshape(n_z, n_z)
     tables = []
-    for table in (forward, swapped, forward.T, swapped.T, basis_y, basis_y.T):
+    for table in (forward, forward.T, basis_y, basis_y.T):
         tables += split_table(np.ascontiguousarray(table))
     s_y = np.broadcast_to(symbol_y[:, None], (n_y, 128)).astype(np.float32)
     s_z = np.tile(symbol_z.reshape(n_narrow, 1, 64), (1, 8, 2)).astype(np.float32)
@@ -387,25 +383,25 @@
     n_wide, n_narrow,
     div, slab, substrate, spread, *rest,
 ):
-    table_refs, rest = rest[:12], rest[12:]
+    table_refs, rest = rest[:8], rest[8:]
     s_y, s_z, press, y_halo, tp, cp = rest[:6]
-    tables, rest = rest[6:18], rest[18:]
+    tables, rest = rest[6:14], rest[14:]
     (
         zsend, rbuf, ubuf, vsend, zrecv, rtab, mom, mrecv, absend, ab, xrecv, yrecv, ysend,
-        first_in, first_sum, second_in, part_xr,
+        relay_in, relay_out, first_in, first_sum, second_in, part_xr,
         nf_send, nf_recv, nb_send, nb_recv, wf_send, wf_recv, wb_send, wb_recv, h_send, h_recv,
-        f_send, f_recv, q_send, q_recv, p_send, p_recv, table_sem, own_sem,
+        f_send, f_recv, q_send, q_recv, p_send, p_recv, table_sem,
     ) = rest
-    fe_h, fe_l, fo_h, fo_l, ie_h, ie_l, io_h, io_l, cy_h, cy_l, iy_h, iy_l = tables
+    fz_h, fz_l, iz_h, iz_l, cy_h, cy_l, iy_h, iy_l = tables
     loads = [
-        pltpu.make_async_copy(table_refs[i], tables[i], table_sem.at[i]) for i in range(12)
+        pltpu.make_async_copy(table_refs[i], tables[i], table_sem.at[i]) for i in range(8)
     ]
 
     def loaded(*which):
         for i in which:
             loads[i].wait()
 
-    for i in (0, 1, 2, 3, 8, 9, 10, 11, 4, 5, 6, 7):
+    for i in (0, 1, 4, 5, 6, 7, 2, 3):
         loads[i].start()
     w = lax.axis_index("wide")
     n = lax.axis_index("narrow")
@@ -428,21 +424,60 @@
         to = lax.rem(own[way] + k, side)
         return (to, to * side + own[1] if way == 0 else own[0] * side + to)
 
-    def first_source(way, to):
-        return slab.at[to, :, pl.ds(0, half)] if way == 0 else slab.at[:, to, pl.ds(half, half)]
-
-    def first_copy(way, k):
-        to, device = peer(way, k)
-        return pltpu.make_async_remote_copy(
-            src_ref=first_source(way, to), dst_ref=first_in.at[way, k],
-            send_sem=f_send.at[way, k], recv_sem=f_recv.at[way, k],
+    quarter = half // 2
+
+    def chunk_rows_of(way, to, part, start=0, size=None):
+        at = pl.ds(way * half + part * quarter + start, quarter if size is None else size)
+        return slab.at[to, :, at] if way == 0 else slab.at[:, to, at]
+
+    def hop(way, direction, source, target, slot):
+        _, device = peer(way, 1 if direction == 0 else side - 1)
+        return pltpu.make_async_remote_copy(
+            src_ref=source, dst_ref=target,
+            send_sem=f_send.at[way, direction, slot], recv_sem=f_recv.at[way, direction, slot],
             device_id=(device, n), device_id_type=MESH,
         )
 
-    def own_first(way):
-        return pltpu.make_async_copy(
-            first_source(way, own[way]), first_in.at[way, 0], own_sem.at[way]
-        )
+    def next_to(way, direction):
+        return peer(way, 1 if direction == 0 else side - 1)[0]
+
+    def far_hop(way, direction):
+        source = chunk_rows_of(way, peer(way, 2)[0], direction)
+        return hop(way, direction, source, relay_in.at[way, direction], 0)
+
+    def near_hop(way, direction):
+        source = chunk_rows_of(way, next_to(way, direction), 1 - direction)
+        target = first_in.at[way, direction, :, pl.ds((1 - direction) * quarter, quarter)]
+        return hop(way, direction, source, target, 1)
+
+    def joint_hop(way, direction):
+        target = first_in.at[way, direction, :, pl.ds(direction * quarter, quarter)]
+        return hop(way, direction, relay_out.at[way, direction], target, 2)
+
+    hops = [(way, direction) for way in (0, 1) for direction in (0, 1)]
+    step = 32
+
+    def relay():
+        for hop_ in hops:
+            far_hop(*hop_).wait_recv()
+        per_slab = quarter // step
+
+        def add(i, c):
+            at = i // per_slab
+            start = pl.multiple_of(lax.rem(i, per_slab) * step, step)
+            here = pl.ds(start, step)
+            for way, direction in hops:
+                to = next_to(way, direction)
+                mine = pl.ds(
+                    pl.multiple_of(way * half + direction * quarter + start, step), step
+                )
+                own_part = slab[to, at, mine] if way == 0 else slab[at, to, mine]
+                relay_out[way, direction, at, here] = relay_in[way, direction, at, here] + own_part
+            return c
+
+        lax.fori_loop(0, side * per_slab, add, 0)
+        for hop_ in hops:
+            joint_hop(*hop_).start()
 
     def second_copy(way, k):
         to, device = peer(1 - way, k)
@@ -455,21 +490,21 @@
     halves = [(way, k) for way in (0, 1) for k in range(1, side)]
 
     def first_total():
-        for way in (0, 1):
-            own_first(way).wait()
-        for way, k in halves:
-            first_copy(way, k).wait_recv()
-        step = 32
+        for hop_ in hops:
+            near_hop(*hop_).wait_recv()
+            joint_hop(*hop_).wait_recv()
         per_slab = half // step
 
         def add(i, c):
             at = i // per_slab
-            here = pl.ds(pl.multiple_of(lax.rem(i, per_slab) * step, step), step)
+            start = pl.multiple_of(lax.rem(i, per_slab) * step, step)
+            here = pl.ds(start, step)
             for way in (0, 1):
-                total = first_in[way, 0, at, here]
-                for k in range(1, side):
-                    total = total + first_in[way, k, at, here]
-                first_sum[way, at, here] = total
+                mine = pl.ds(pl.multiple_of(way * half + start, step), step)
+                total = slab[own[0], at, mine] if way == 0 else slab[at, own[1], mine]
+                first_sum[way, at, here] = (
+                    total + first_in[way, 0, at, here] + first_in[way, 1, at, here]
+                )
             return c
 
         lax.fori_loop(0, side * per_slab, add, 0)
@@ -578,17 +613,15 @@
             device_id=(w, source), device_id_type=MESH,
         )
 
-    for way in (0, 1):
-        own_first(way).start()
-    loaded(0, 1, 2, 3)
+    loaded(0, 1)
     for g in range(GROUPS):
-        even = div[g * per:(g + 1) * per, 0].reshape(per * rows, n_z)
-        odd = div[g * per:(g + 1) * per, 1].reshape(per * rows, n_z)
-        even = dot_left(even, fe_h[...], fe_l[...])
-        odd = dot_left(odd, fo_h[...], fo_l[...])
+        lines = div[g * per:(g + 1) * per].reshape(per * 2 * rows, n_z)
+        lines = dot_left(lines, fz_h[...], fz_l[...]).reshape(per, 2, rows, n_z)
+        even = lines[:, 0].reshape(per * rows, n_z)
+        odd = lines[:, 1].reshape(per * rows, n_z)
         for m in range(n_z // 128):
             e = even[:, 128 * m:128 * (m + 1)]
-            o = odd[:, 128 * m:128 * (m + 1)]
+            o = pltpu.roll(odd[:, 128 * m:128 * (m + 1)], 64, 1)
             first = jnp.where(low_half, e, o)
             second = jnp.where(low_half, o, e)
             zsend[2 * m, g * per:(g + 1) * per] = first.reshape(per, rows, 128)
@@ -602,11 +635,13 @@
 
         lax.fori_loop(1, n_narrow, launch, 0)
         if g == 0:
-            for way, k in halves:
-                first_copy(way, k).start()
+            for hop_ in hops:
+                far_hop(*hop_).start()
             cp[DEEP:DEEP + planes, PAD:PAD + part_rows] = spread[...]
             part_x_start(cp, 1)
 
+    for hop_ in hops:
+        near_hop(*hop_).start()
     s = s_y[...] + s_z[n][0:1, :] + penalty
     root = jnp.sqrt(s * (1.0 + s))
     rtab[0] = 1.0 / (1.0 + 2.0 * s + 2.0 * root)
@@ -617,7 +652,8 @@
         rbuf[span, pl.ds(pl.multiple_of(n * rows, rows), rows)] = zsend[n, span]
         if g == 0:
             part_x_end(cp, 1)
-            loaded(8, 9)
+            relay()
+            loaded(4, 5)
 
         def arrive(k, c):
             forward_arrival(g, k).wait_recv()
@@ -749,7 +785,7 @@
             device_id=(w, source), device_id_type=MESH,
         )
 
-    loaded(10, 11)
+    loaded(6, 7)
     for g in range(GROUPS):
         span = slice(g * per, (g + 1) * per)
         lines = jnp.concatenate([ubuf[xp] for xp in range(g * per, (g + 1) * per)], axis=1)
@@ -762,7 +798,7 @@
 
     first_total()
     part_y_end(cp, 1)
-    loaded(4, 5, 6, 7)
+    loaded(2, 3)
 
     def x_halo(side):
         source = 2 * xps if side else 1
@@ -786,9 +822,12 @@
             first = zrecv[2 * m, g * per:(g + 1) * per].reshape(per * rows, 128)
             second = zrecv[2 * m + 1, g * per:(g + 1) * per].reshape(per * rows, 128)
             evens.append(jnp.where(low_half, first, second))
-            odds.append(jnp.where(low_half, second, first))
-        even = dot_left(jnp.concatenate(evens, axis=1), ie_h[...], ie_l[...])
-        odd = dot_left(jnp.concatenate(odds, axis=1), io_h[...], io_l[...])
+            odds.append(pltpu.roll(jnp.where(low_half, second, first), 64, 1))
+        lines = jnp.concatenate(
+            [jnp.concatenate(evens, axis=1), jnp.concatenate(odds, axis=1)], axis=0
+        )
+        lines = dot_left(lines, iz_h[...], iz_l[...])
+        even, odd = lines[:per * rows], lines[per * rows:]
         for i in range(per):
             for parity, part in ((0, even), (1, odd)):
                 x = 2 * (g * per + i) + parity
@@ -805,8 +844,11 @@
     part_x_end(tp, 0)
 
     for way, k in halves:
-        first_copy(way, k).wait_send()
         second_copy(way, k).wait_send()
+    for hop_ in hops:
+        far_hop(*hop_).wait_send()
+        near_hop(*hop_).wait_send()
+        joint_hop(*hop_).wait_send()
     for g in range(GROUPS):
         each(n_narrow, lambda k: forward_copy(g, k).wait_send())
         each(n_narrow, lambda k: backward_copy(g, k).wait_send())
@@ -844,9 +886,9 @@
             jax.ShapeDtypeStruct(part, F32),
             jax.ShapeDtypeStruct(part, F32),
         ],
-        in_specs=[VM, any_space, VM, VM] + [any_space] * 12 + [VM, VM],
+        in_specs=[VM, VM, VM, VM] + [any_space] * 8 + [VM, VM],
         out_specs=[VM] * 4,
-        scratch_shapes=[pltpu.VMEM(t.shape, BF16) for t in tables[:12]]
+        scratch_shapes=[pltpu.VMEM(t.shape, BF16) for t in tables[:8]]
         + [
             pltpu.VMEM(turned, F32),
             pltpu.VMEM(field, F32),
@@ -861,7 +903,9 @@
             pltpu.VMEM((2, rows, n_z), F32),
             pltpu.VMEM((2, x_local, n_z), F32),
             pltpu.VMEM((2, x_local, n_z), F32),
-            pltpu.VMEM((2, side, side, half, depth), F32),
+            pltpu.VMEM((2, 2, side, half // 2, depth), F32),
+            pltpu.VMEM((2, 2, side, half // 2, depth), F32),
+            pltpu.VMEM((2, 2, side, half, depth), F32),
             pltpu.VMEM((2, side, half, depth), F32),
             pltpu.VMEM((2, side, half, depth), F32),
             pltpu.VMEM((2, 2, DEEP, part_rows, depth), F32),
@@ -875,17 +919,16 @@
             dma((n_wide,)),
             dma((4,)),
             dma((4,)),
-            dma((2, side)),
-            dma((2, side)),
+            dma((2, 2, 3)),
+            dma((2, 2, 3)),
             dma((2, side)),
             dma((2, side)),
             dma((2, 4)),
             dma((2, 4)),
-            dma((12,)),
-            dma((2,)),
+            dma((8,)),
         ],
         compiler_params=pltpu.CompilerParams(
-            collective_id=1, has_side_effects=True, vmem_limit_bytes=52 * 2**20
+            collective_id=1, has_side_effects=True, vmem_limit_bytes=32 * 2**20
         ),
         name="pressure",
     )(
@@ -895,14 +938,13 @@
     )
 
 
-def conduct(step, source, coefficient, target):
+def conduct(step, span, source, coefficient, target):
     planes, rows, depth = coefficient.shape
     lane = lax.broadcasted_iota(jnp.int32, (rows, depth), 1)
 
-    def plane(x, below):
+    def plane(x, c):
         p = source[x]
-        above = source[x + 1]
-        around = above + below + pltpu.roll(p, 1, 0) + pltpu.roll(p, rows - 1, 0)
+        around = source[x + 1] + source[x - 1] + pltpu.roll(p, 1, 0) + pltpu.roll(p, rows - 1, 0)
         around += jnp.where(lane == 0, 0.0, pltpu.roll(p, 1, 1))
         around += jnp.where(lane == depth - 1, 0.0, pltpu.roll(p, depth - 1, 1))
         new = p + coefficient[x] * (around - 6.0 * p)
@@ -910,9 +952,9 @@
             target[x - DEEP] = new[PAD:rows - PAD]
         else:
             target[x] = new
-        return p
-
-    lax.fori_loop(step + 1, planes - step - 1, plane, source[step])
+        return c
+
+    lax.fori_loop(*span, plane, 0, unroll=2)
 
 
 def y_step(plane, before, after, ahead):
@@ -923,21 +965,25 @@
     return jnp.where(row == 0, before, pltpu.roll(plane, 1, 0))
 
 
-def project_kernel(press, y_halo, tp, cp, current, out, part, tq):
+def project_kernel(lead, trail, y_halo, tp, cp, current, out, part, tq, tr):
     step = pl.program_id(0)
-    n_z = press.shape[2]
-    for i in range(STEPS):
+    planes, n_z = current.shape[1], current.shape[3]
+    total = tp.shape[0]
+    for i in range(2 * STEPS):
 
         @pl.when(step == i)
         def _():
-            conduct(i, (tp, tq, tq)[i], cp, (tq, tq, part)[i])
-
-    for i in range(current.shape[1]):
-        x = step * current.shape[1] + i
-        p = press[x + 1]
+            first, last = i // 2 + 1, total - i // 2 - 1
+            span = (first, total // 2) if i % 2 == 0 else (total // 2, last)
+            conduct(i // 2, span, (tp, tq, tr)[i // 2], cp, (tq, tr, part)[i // 2])
+
+    block = [lead[0], lead[1], trail[0], trail[1]]
+    for i in range(planes):
+        x = step * planes + i
+        p = block[i + 1]
         before = y_halo[0, pl.ds(x, 1)]
         after = y_halo[1, pl.ds(x, 1)]
-        out[0, i] = current[0, i] - (press[x + 2] - press[x]) * 0.5
+        out[0, i] = current[0, i] - (block[i + 2] - block[i]) * 0.5
         out[1, i] = current[1, i] - 0.5 * (
             y_step(p, before, after, True) - y_step(p, before, after, False)
         )
@@ -953,12 +999,16 @@
         project_kernel,
         grid=(x_local // planes,),
         out_shape=[jax.ShapeDtypeStruct(current.shape, F32), jax.ShapeDtypeStruct(part, F32)],
-        in_specs=[VM, VM, VM, VM, spec],
+        in_specs=[
+            pl.BlockSpec((planes, rows, n_z), lambda i: (i, 0, 0)),
+            pl.BlockSpec((planes, rows, n_z), lambda i: (i + 1, 0, 0)),
+            VM, VM, VM, spec,
+        ],
         out_specs=[spec, pl.BlockSpec(part, lambda i: (0, 0, 0))],
-        scratch_shapes=[pltpu.VMEM(tp.shape, F32)],
+        scratch_shapes=[pltpu.VMEM(tp.shape, F32), pltpu.VMEM(tp.shape, F32)],
         compiler_params=pltpu.CompilerParams(vmem_limit_bytes=20 * 2**20),
         name="projection",
-    )(press, y_halo, tp, cp, current)
+    )(press, press, y_halo, tp, cp, current)
 
 
 def per_device(

time: 136 us -> 113 us (0.83)
  Pallas kernels: 126 us -> 109 us
  local copies, waits for them, and re-layouts: 6.61 us -> 1.31 us
    pallas_call x1, Pallas kernels: 66.2 us -> 53.4 us  [solve_pressure(): pl.pallas_call(functools.partial(pressure_kernel, n_wide, n_narrow), out_...]
    unnamed x32 -> x28, local copies, waits for them, and re-layouts: 6.61 us -> 1.31 us
    pallas_call x1, Pallas kernels: 45.7 us -> 43.2 us  [flow(): pl.pallas_call(functools.partial(flow_kernel, n_wide, n_narrow), out_shap...]
    pallas_call x1, Pallas kernels: 7.98 us -> 5.86 us  [project(): pl.pallas_call(project_kernel, grid=(x_local // planes,), out_shape=[jax....]
where the time goes in v2:
time: 113 us
  Pallas kernels  109 us (96%)
  other arithmetic  1.4 us (1%)
  local copies, waits for them, and re-layouts  1.31 us (1%)
    pallas_call x1, Pallas kernels, solve_pressure(): pl.pallas_call(functools.partial(pressure_kernel, n_wide, n_narrow), out_...  53.4 us
    pallas_call x1, Pallas kernels, flow(): pl.pallas_call(functools.partial(flow_kernel, n_wide, n_narrow), out_shap...  43.2 us
    pallas_call x1, Pallas kernels, slab_heat(): pl.pallas_call(gather_kernel, out_shape=jax.ShapeDtypeStruct((lines, 128)...  6.45 us
    pallas_call x1, Pallas kernels, project(): pl.pallas_call(project_kernel, grid=(x_local // planes,), out_shape=[jax....  5.86 us

profile of v2, /device:TPU:1, one launch (start us, length us, event | category | flops | bytes accessed | tf_op | source)
XLA Modules:
  0.0 112.5 jit_solution(16384454369503914374)
XLA Ops:
  0.6 0.7 broadcast_multiply_fusion
  1.3 0.7 add.3.target
  2.0 1.2 %copy-done.1 = f32[16,32,512]{2,1,0:T(8,128)S(1)} copy-done((f32[16,32,512]{2,1,0:T(8,128)S(1)}, f32[16,32,512]{2,1,0:T(8,128)}, u32[]{:S(2)}) %copy-start.1) | copy-done | bytes 1048600
  3.3 43.2 %flow.1 = (f32[3,16,32,512]{3,2,1,0:T(8,128)}, f32[16,32,512]{2,1,0:T(8,128)S(1)}, f32[4,512,128]{2,1,0:T(8,128)S(1)}) custom-call(f32[3,16,32,512]{3,2,1,0:T(8,128)} %vel_in.1, f32[3,16,32,512]{3,2,1,0:T(8,128)} %push_in.1, f32[16,32,512]{2,1,0:T(8,128)S(1)} %copy-done.1), custom_call_target="tpu_custom_call" | custom-call | tf_op jit(solution)/shard_map/flow/pallas_call | solution.py:280
  46.5 0.0 copy-start.2
  46.5 0.0 copy-start.3
  46.5 0.0 copy-start.4
  46.5 0.0 copy-start.5
  46.5 0.0 copy-start.6
  46.5 0.0 copy-start.7
  46.5 0.0 copy-start.8
  46.6 0.0 copy-start.9
  46.6 0.0 copy-start.10
  46.6 0.0 copy-start.11
  46.6 0.0 copy-start.12
  46.6 0.0 copy-start.13
  46.6 6.4 %slab_heat.1 = f32[8192,128]{1,0:T(8,128)S(1)} custom-call(s32[2048]{0:T(1024)S(1)} %add.3.target, f32[4,512,128]{2,1,0:T(8,128)S(1)} %get-tuple-element.10.heat), custom_call_target="tpu_custom_call" | custom-call | tf_op jit(solution)/shard_map/slab_heat/pallas_call | solution.py:322
  53.1 0.0 copy-done.2
  53.1 0.0 copy-done.3
  53.1 0.0 copy-done.4
  53.1 0.0 copy-done.5
  53.1 0.0 copy-done.6
  53.1 0.0 copy-done.7
  53.1 0.0 copy-done.8
  53.1 0.0 copy-done.9
  53.2 0.0 copy-done.10
  53.2 0.0 copy-done.11
  53.2 0.0 copy-done.12
  53.2 0.0 copy-done.13
  53.2 0.0 copy-start
  53.2 53.4 %pressure.1 = (f32[18,32,512]{2,1,0:T(8,128)S(1)}, f32[2,16,512]{2,1,0:T(8,128)S(1)}, f32[22,48,128]{2,1,0:T(8,128)S(1)}, f32[22,48,128]{2,1,0:T(8,128)S(1)}) custom-call(f32[8,2,32,512]{3,2,1,0:T(8,128)S(1)} %bitcast.4, f32[4,4,512,128]{3,2,1,0:T(8,128)S(1)} %bitcast.3, f32[16,32,128]{2,1,0:T(8,128)S(1)} %copy-done.6, f32[16,32,128]{2,1,0:T(8,128)S(1)} %copy-done.7, ...), custom_call_target="tpu_custom_call" | custom-call | tf_op jit(solution)/shard_map/pressure/pallas_call | solution.py:881
  106.7 5.9 %projection.1 = (f32[3,16,32,512]{3,2,1,0:T(8,128)}, f32[16,32,128]{2,1,0:T(8,128)}) custom-call(f32[18,32,512]{2,1,0:T(8,128)S(1)} %get-tuple-element.11.lead.trail, f32[18,32,512]{2,1,0:T(8,128)S(1)} %get-tuple-element.11.lead.trail, f32[2,16,512]{2,1,0:T(8,128)S(1)} %get-tuple-element.12.y_halo, f32[22,48,128]{2,1,0:T(8,128)S(1)} %get-tuple-element.13.tp, ...), custom_call_target="tpu_custom_call" | custom-call | tf_op jit(solution)/shard_map/projection/pallas_call | solution.py:998
  (2 shorter events, 0.0 us)
Async XLA Ops:
  2.0 1.2 %copy-start.1 = (f32[16,32,512]{2,1,0:T(8,128)S(1)}, f32[16,32,512]{2,1,0:T(8,128)}, u32[]{:S(2)}) copy-start(f32[16,32,512]{2,1,0:T(8,128)} %warmth_in.1) | copy-start | bytes 3145732
  46.5 6.6 %copy-start.2 = (bf16[512,512]{1,0:T(8,128)(2,1)S(1)}, bf16[512,512]{1,0:T(8,128)(2,1)}, u32[]{:S(2)}) copy-start(bf16[512,512]{1,0:T(8,128)(2,1)} %constant.25.clone.rest_3_) | copy-start | bytes 1572868
  46.5 6.6 %copy-start.3 = (bf16[512,512]{1,0:T(8,128)(2,1)S(1)}, bf16[512,512]{1,0:T(8,128)(2,1)}, u32[]{:S(2)}) copy-start(bf16[512,512]{1,0:T(8,128)(2,1)} %constant.24.clone.rest_2_) | copy-start | bytes 1572868
  46.5 6.6 %copy-start.4 = (bf16[512,512]{1,0:T(8,128)(2,1)S(1)}, bf16[512,512]{1,0:T(8,128)(2,1)}, u32[]{:S(2)}) copy-start(bf16[512,512]{1,0:T(8,128)(2,1)} %constant.23.clone.rest_1_) | copy-start | bytes 1572868
  46.5 6.6 %copy-start.5 = (bf16[512,512]{1,0:T(8,128)(2,1)S(1)}, bf16[512,512]{1,0:T(8,128)(2,1)}, u32[]{:S(2)}) copy-start(bf16[512,512]{1,0:T(8,128)(2,1)} %constant.22.clone.rest_0_) | copy-start | bytes 1572868
  46.5 6.6 %copy-start.6 = (f32[16,32,128]{2,1,0:T(8,128)S(1)}, f32[16,32,128]{2,1,0:T(8,128)}, u32[]{:S(2)}) copy-start(f32[16,32,128]{2,1,0:T(8,128)} %substrate.1) | copy-start | bytes 786436
  46.5 6.6 %copy-start.7 = (f32[16,32,128]{2,1,0:T(8,128)S(1)}, f32[16,32,128]{2,1,0:T(8,128)}, u32[]{:S(2)}) copy-start(f32[16,32,128]{2,1,0:T(8,128)} %spread.1) | copy-start | bytes 786436
  46.5 6.6 %copy-start.8 = (f32[256,128]{1,0:T(8,128)S(1)}, f32[256,128]{1,0:T(8,128)}, u32[]{:S(2)}) copy-start(f32[256,128]{1,0:T(8,128)} %constant.30.clone.rest_8_) | copy-start | bytes 393220
  46.6 6.6 %copy-start.9 = (bf16[256,256]{1,0:T(8,128)(2,1)S(1)}, bf16[256,256]{1,0:T(8,128)(2,1)}, u32[]{:S(2)}) copy-start(bf16[256,256]{1,0:T(8,128)(2,1)} %constant.29.clone.rest_7_) | copy-start | bytes 393220
  46.6 6.6 %copy-start.10 = (bf16[256,256]{1,0:T(8,128)(2,1)S(1)}, bf16[256,256]{1,0:T(8,128)(2,1)}, u32[]{:S(2)}) copy-start(bf16[256,256]{1,0:T(8,128)(2,1)} %constant.28.clone.rest_6_) | copy-start | bytes 393220
  46.6 6.6 %copy-start.11 = (bf16[256,256]{1,0:T(8,128)(2,1)S(1)}, bf16[256,256]{1,0:T(8,128)(2,1)}, u32[]{:S(2)}) copy-start(bf16[256,256]{1,0:T(8,128)(2,1)} %constant.27.clone.rest_5_) | copy-start | bytes 393220
  46.6 6.6 %copy-start.12 = (bf16[256,256]{1,0:T(8,128)(2,1)S(1)}, bf16[256,256]{1,0:T(8,128)(2,1)}, u32[]{:S(2)}) copy-start(bf16[256,256]{1,0:T(8,128)(2,1)} %constant.26.clone.rest_4_) | copy-start | bytes 393220
  46.6 6.6 %copy-start.13 = (f32[8,8,128]{2,1,0:T(8,128)S(1)}, f32[8,8,128]{2,1,0:T(8,128)}, u32[]{:S(2)}) copy-start(f32[8,8,128]{2,1,0:T(8,128)} %constant.31.clone.rest_9_) | copy-start | bytes 98308
  53.2 53.5 %copy-start = (f32[3,16,32,512]{3,2,1,0:T(8,128)S(1)}, f32[3,16,32,512]{3,2,1,0:T(8,128)}, u32[]{:S(2)}) copy-start(f32[3,16,32,512]{3,2,1,0:T(8,128)} %get-tuple-element.15.current) | copy-start | bytes 9437188

commit v3 on v2

--- a/solution.py
+++ b/solution.py
@@ -81,12 +81,12 @@
     def y_pair(e, sends, lands):
         return [narrow_copy(e, side, sends, lands) for side in (0, 1)]
 
-    def all_x(action, first=0, last=None):
+    def all_x(action, first=0, last=None, unroll=1):
         def step(x, c):
             action(x)
             return c
 
-        lax.fori_loop(first, planes if last is None else last, step, 0)
+        lax.fori_loop(first, planes if last is None else last, step, 0, unroll=unroll)
 
     def y_fill(field, lands, comps):
         def fill(x):
@@ -198,11 +198,11 @@
         return plane
 
     def stage(action, arriving_x, arriving_y, fill, fill_x=None):
-        all_x(lambda x: action(x, range(1, strips - 1)), 1, planes - 1)
+        all_x(lambda x: action(x, range(1, strips - 1)), 1, planes - 1, 2)
         for copy in arriving_y:
             copy.wait_recv()
         fill()
-        all_x(lambda x: action(x, (0, strips - 1)), 1, planes - 1)
+        all_x(lambda x: action(x, (0, strips - 1)), 1, planes - 1, 2)
         for copy in arriving_x:
             copy.wait_recv()
         if fill_x is not None:
@@ -387,7 +387,7 @@
     s_y, s_z, press, y_halo, tp, cp = rest[:6]
     tables, rest = rest[6:14], rest[14:]
     (
-        zsend, rbuf, ubuf, vsend, zrecv, rtab, mom, mrecv, absend, ab, xrecv, yrecv, ysend,
+        zsend, rbuf, ubuf, vsend, zrecv, rtab, halves_, mom, mrecv, absend, ab, xrecv, yrecv, ysend,
         relay_in, relay_out, first_in, first_sum, second_in, part_xr,
         nf_send, nf_recv, nb_send, nb_recv, wf_send, wf_recv, wb_send, wb_recv, h_send, h_recv,
         f_send, f_recv, q_send, q_recv, p_send, p_recv, table_sem,
@@ -407,7 +407,7 @@
     n = lax.axis_index("narrow")
     xps, _, rows, n_z = div.shape
     n_y = s_y.shape[0]
-    per = xps // GROUPS
+    per = xps // 2
     chunk_rows = n_y // n_wide
 
     def across(k):
@@ -593,6 +593,20 @@
 
     lane = lax.broadcasted_iota(jnp.int32, (per * rows, 128), 1)
     low_half = lane < 64
+    odd = lax.rem(n, 2)
+    block = 16
+
+    def later_half(count):
+        lanes = lax.broadcasted_iota(jnp.int32, (count, 128), 1)
+        return jnp.where(lanes < 64, odd, 1 - odd) == 1
+
+    def swap(x):
+        return pltpu.roll(x, 64, 1)
+
+    def power(x, exponent):
+        for _ in range(int(math.log2(exponent))):
+            x = x * x
+        return x
 
     def forward_copy(g, k):
         to = across(k)
@@ -615,13 +629,11 @@
 
     loaded(0, 1)
     for g in range(GROUPS):
-        lines = div[g * per:(g + 1) * per].reshape(per * 2 * rows, n_z)
-        lines = dot_left(lines, fz_h[...], fz_l[...]).reshape(per, 2, rows, n_z)
-        even = lines[:, 0].reshape(per * rows, n_z)
-        odd = lines[:, 1].reshape(per * rows, n_z)
+        lines = div[:, g].reshape(xps * rows, n_z)
+        lines = dot_left(lines, fz_h[...], fz_l[...])
         for m in range(n_z // 128):
-            e = even[:, 128 * m:128 * (m + 1)]
-            o = pltpu.roll(odd[:, 128 * m:128 * (m + 1)], 64, 1)
+            e = lines[:per * rows, 128 * m:128 * (m + 1)]
+            o = swap(lines[per * rows:, 128 * m:128 * (m + 1)])
             first = jnp.where(low_half, e, o)
             second = jnp.where(low_half, o, e)
             zsend[2 * m, g * per:(g + 1) * per] = first.reshape(per, rows, 128)
@@ -647,124 +659,99 @@
     rtab[0] = 1.0 / (1.0 + 2.0 * s + 2.0 * root)
     rtab[1] = -1.0 / root
 
+    def chunk(index):
+        return pl.ds(pl.multiple_of(index * chunk_rows, chunk_rows), chunk_rows)
+
+    def out_copy(g, k):
+        to = along(k)
+        return pltpu.make_async_remote_copy(
+            src_ref=mom.at[g, chunk(to)], dst_ref=mrecv.at[g, w],
+            send_sem=wf_send.at[g, k], recv_sem=wf_recv.at[g, k],
+            device_id=(to, n), device_id_type=MESH,
+        )
+
+    def out_arrival(g, k):
+        here = mrecv.at[g, along(n_wide - k)]
+        return pltpu.make_async_remote_copy(
+            src_ref=here, dst_ref=here, send_sem=wf_send.at[g, k], recv_sem=wf_recv.at[g, k],
+            device_id=(along(n_wide - k), n), device_id_type=MESH,
+        )
+
+    def back_copy(g, k):
+        to = along(k)
+        return pltpu.make_async_remote_copy(
+            src_ref=absend.at[g, to], dst_ref=ab.at[g, chunk(w)],
+            send_sem=wb_send.at[g, k], recv_sem=wb_recv.at[g, k],
+            device_id=(to, n), device_id_type=MESH,
+        )
+
+    def back_arrival(g, k):
+        here = ab.at[g, chunk(along(n_wide - k))]
+        return pltpu.make_async_remote_copy(
+            src_ref=here, dst_ref=here, send_sem=wb_send.at[g, k], recv_sem=wb_recv.at[g, k],
+            device_id=(along(n_wide - k), n), device_id_type=MESH,
+        )
+
+    def each(count, action):
+        def body(k, c):
+            action(k)
+            return c
+
+        lax.fori_loop(1, count, body, 0)
+
     for g in range(GROUPS):
         span = slice(g * per, (g + 1) * per)
         rbuf[span, pl.ds(pl.multiple_of(n * rows, rows), rows)] = zsend[n, span]
         if g == 0:
             part_x_end(cp, 1)
-            relay()
             loaded(4, 5)
-
-        def arrive(k, c):
-            forward_arrival(g, k).wait_recv()
-            return c
-
-        lax.fori_loop(1, n_narrow, arrive, 0)
-        lines = jnp.concatenate([rbuf[xp] for xp in range(g * per, (g + 1) * per)], axis=1)
+        each(n_narrow, lambda k: forward_arrival(g, k).wait_recv())
+        lines = jnp.concatenate([rbuf[i] for i in range(g * per, (g + 1) * per)], axis=1)
         lines = dot_right(cy_h[...], cy_l[...], lines)
         for i in range(per):
             ubuf[g * per + i] = lines[:, 128 * i:128 * (i + 1)]
 
-    block = 16
-
-    def moments(i, c):
-        here = pl.ds(pl.multiple_of(i * block, block), block)
-        r = rtab[0, here]
-        f = ubuf[0, here]
-        b = ubuf[xps - 1, here]
-        for xp in range(1, xps):
-            f = f * r + ubuf[xp, here]
-            b = b * r + ubuf[xps - 1 - xp, here]
-        mom[0, here] = f
-        mom[1, here] = b
-        return c
-
-    lax.fori_loop(0, n_y // block, moments, 0)
-
-    def chunk(index):
-        return pl.ds(pl.multiple_of(index * chunk_rows, chunk_rows), chunk_rows)
-
-    def out_copy(k):
-        to = along(k)
-        return pltpu.make_async_remote_copy(
-            src_ref=mom.at[:, chunk(to)], dst_ref=mrecv.at[w],
-            send_sem=wf_send.at[k], recv_sem=wf_recv.at[k],
-            device_id=(to, n), device_id_type=MESH,
-        )
-
-    def out_arrival(k):
-        here = mrecv.at[along(n_wide - k)]
-        return pltpu.make_async_remote_copy(
-            src_ref=here, dst_ref=here, send_sem=wf_send.at[k], recv_sem=wf_recv.at[k],
-            device_id=(along(n_wide - k), n), device_id_type=MESH,
-        )
-
-    def back_copy(k):
-        to = along(k)
-        return pltpu.make_async_remote_copy(
-            src_ref=absend.at[to], dst_ref=ab.at[:, chunk(w)],
-            send_sem=wb_send.at[k], recv_sem=wb_recv.at[k],
-            device_id=(to, n), device_id_type=MESH,
-        )
-
-    def back_arrival(k):
-        here = ab.at[:, chunk(along(n_wide - k))]
-        return pltpu.make_async_remote_copy(
-            src_ref=here, dst_ref=here, send_sem=wb_send.at[k], recv_sem=wb_recv.at[k],
-            device_id=(along(n_wide - k), n), device_id_type=MESH,
-        )
-
-    def each(count, action):
-        def body(k, c):
-            action(k)
+        def moments(i, c):
+            here = pl.ds(pl.multiple_of(i * block, block), block)
+            r = rtab[0, here]
+            f = ubuf[g * per, here]
+            b = ubuf[g * per + per - 1, here]
+            for k in range(1, per):
+                f = f * r + ubuf[g * per + k, here]
+                b = b * r + ubuf[g * per + per - 1 - k, here]
+            halves_[g, 0, here] = f
+            halves_[g, 1, here] = b
+            rp = power(r, per)
+            mom[g, here] = jnp.where(later_half(block), f + rp * swap(f), b + rp * swap(b))
             return c
 
-        lax.fori_loop(1, count, body, 0)
-
-    each(n_wide, lambda k: out_copy(k).start())
-    mrecv[w] = mom[:, chunk(w)]
-    r = rtab[0, chunk(w)]
-    q = r
-    for _ in range(int(math.log2(xps))):
-        q = q * q
-    total = q
-    for _ in range(int(math.log2(n_wide))):
-        total = total * total
-    closing = 1.0 / (1.0 - total)
-    each(n_wide, lambda k: out_arrival(k).wait_recv())
-    f = mrecv[0, 0]
-    b = mrecv[n_wide - 1, 1]
-    for j in range(1, n_wide):
-        f = f * q + mrecv[j, 0]
-        b = b * q + mrecv[n_wide - 1 - j, 1]
-    f = f * closing
-    b = b * closing
-    for j in range(n_wide):
-        absend[j, 0] = f
-        absend[n_wide - 1 - j, 1] = b
-        f = f * q + mrecv[j, 0]
-        b = b * q + mrecv[n_wide - 1 - j, 1]
-    each(n_wide, lambda k: back_copy(k).start())
-    ab[:, chunk(w)] = absend[w]
-    each(n_wide, lambda k: back_arrival(k).wait_recv())
-
-    def solve(i, c):
-        here = pl.ds(pl.multiple_of(i * block, block), block)
-        r = rtab[0, here]
-        scale = rtab[1, here]
-        f = ab[0, here]
-        b = ab[1, here]
-        behind = []
-        for xp in range(xps - 1, -1, -1):
-            rb = b * r
-            behind.append(rb)
-            b = rb + ubuf[xp, here]
-        for xp in range(xps):
-            f = f * r + ubuf[xp, here]
-            ubuf[xp, here] = scale * (f + behind[xps - 1 - xp])
-        return c
-
-    lax.fori_loop(0, n_y // block, solve, 0)
+        lax.fori_loop(0, n_y // block, moments, 0)
+        each(n_wide, lambda k: out_copy(g, k).start())
+        mrecv[g, w] = mom[g, chunk(w)]
+        if g == 0:
+            relay()
+
+    q = power(rtab[0, chunk(w)], xps)
+    closing = 1.0 / (1.0 - power(q, n_wide))
+    for g in range(GROUPS):
+        each(n_wide, lambda k: out_arrival(g, k).wait_recv())
+        f = mrecv[g, 0]
+        b = mrecv[g, n_wide - 1]
+        for j in range(1, n_wide):
+            f = f * q + mrecv[g, j]
+            b = b * q + mrecv[g, n_wide - 1 - j]
+        f = f * closing
+        b = b * closing
+        ahead, behind = [], []
+        for j in range(n_wide):
+            ahead.append(f)
+            behind.append(b)
+            f = f * q + mrecv[g, j]
+            b = b * q + mrecv[g, n_wide - 1 - j]
+        for j in range(n_wide):
+            absend[g, j] = jnp.where(later_half(chunk_rows), ahead[j], behind[n_wide - 1 - j])
+        each(n_wide, lambda k: back_copy(g, k).start())
+        ab[g, chunk(w)] = absend[g, w]
 
     def backward_copy(g, k):
         to = across(k)
@@ -788,7 +775,32 @@
     loaded(6, 7)
     for g in range(GROUPS):
         span = slice(g * per, (g + 1) * per)
-        lines = jnp.concatenate([ubuf[xp] for xp in range(g * per, (g + 1) * per)], axis=1)
+        each(n_wide, lambda k: back_arrival(g, k).wait_recv())
+
+        def solve(i, c):
+            here = pl.ds(pl.multiple_of(i * block, block), block)
+            later = later_half(block)
+            r = rtab[0, here]
+            scale = rtab[1, here]
+            rp = power(r, per)
+            mixed = ab[g, here]
+            other = swap(mixed)
+            f = jnp.where(later, mixed, other)
+            b = jnp.where(later, other, mixed)
+            f = jnp.where(later, rp * f + swap(halves_[g, 0, here]), f)
+            b = jnp.where(later, b, rp * b + swap(halves_[g, 1, here]))
+            behind = []
+            for k in range(per - 1, -1, -1):
+                rb = b * r
+                behind.append(rb)
+                b = rb + ubuf[g * per + k, here]
+            for k in range(per):
+                f = f * r + ubuf[g * per + k, here]
+                ubuf[g * per + k, here] = scale * (f + behind[per - 1 - k])
+            return c
+
+        lax.fori_loop(0, n_y // block, solve, 0)
+        lines = jnp.concatenate([ubuf[i] for i in range(g * per, (g + 1) * per)], axis=1)
         lines = dot_right(iy_h[...], iy_l[...], lines)
         for to in range(n_narrow):
             for i in range(per):
@@ -822,19 +834,17 @@
             first = zrecv[2 * m, g * per:(g + 1) * per].reshape(per * rows, 128)
             second = zrecv[2 * m + 1, g * per:(g + 1) * per].reshape(per * rows, 128)
             evens.append(jnp.where(low_half, first, second))
-            odds.append(pltpu.roll(jnp.where(low_half, second, first), 64, 1))
+            odds.append(swap(jnp.where(low_half, second, first)))
         lines = jnp.concatenate(
             [jnp.concatenate(evens, axis=1), jnp.concatenate(odds, axis=1)], axis=0
         )
         lines = dot_left(lines, iz_h[...], iz_l[...])
-        even, odd = lines[:per * rows], lines[per * rows:]
-        for i in range(per):
-            for parity, part in ((0, even), (1, odd)):
-                x = 2 * (g * per + i) + parity
-                plane = part[i * rows:(i + 1) * rows]
-                press[x + 1] = plane
-                ysend[0, x] = plane[0]
-                ysend[1, x] = plane[rows - 1]
+        for i in range(xps):
+            plane = lines[i * rows:(i + 1) * rows]
+            x = 2 * i + g
+            press[x + 1] = plane
+            ysend[0, x] = plane[0]
+            ysend[1, x] = plane[rows - 1]
         if g == 0:
             x_halo(0).start()
             part_start()
@@ -852,8 +862,8 @@
     for g in range(GROUPS):
         each(n_narrow, lambda k: forward_copy(g, k).wait_send())
         each(n_narrow, lambda k: backward_copy(g, k).wait_send())
-    each(n_wide, lambda k: out_copy(k).wait_send())
-    each(n_wide, lambda k: back_copy(k).wait_send())
+        each(n_wide, lambda k: out_copy(g, k).wait_send())
+        each(n_wide, lambda k: back_copy(g, k).wait_send())
     for side in (0, 1):
         x_halo(side).wait()
         y_halo_copy(side).wait()
@@ -896,10 +906,11 @@
             pltpu.VMEM(turned, F32),
             pltpu.VMEM(turned, F32),
             pltpu.VMEM((2, n_y, 128), F32),
-            pltpu.VMEM((2, n_y, 128), F32),
-            pltpu.VMEM((n_wide, 2, chunk_rows, 128), F32),
-            pltpu.VMEM((n_wide, 2, chunk_rows, 128), F32),
-            pltpu.VMEM((2, n_y, 128), F32),
+            pltpu.VMEM((GROUPS, 2, n_y, 128), F32),
+            pltpu.VMEM((GROUPS, n_y, 128), F32),
+            pltpu.VMEM((GROUPS, n_wide, chunk_rows, 128), F32),
+            pltpu.VMEM((GROUPS, n_wide, chunk_rows, 128), F32),
+            pltpu.VMEM((GROUPS, n_y, 128), F32),
             pltpu.VMEM((2, rows, n_z), F32),
             pltpu.VMEM((2, x_local, n_z), F32),
             pltpu.VMEM((2, x_local, n_z), F32),
@@ -913,10 +924,10 @@
             dma((GROUPS, n_narrow)),
             dma((GROUPS, n_narrow)),
             dma((GROUPS, n_narrow)),
-            dma((n_wide,)),
-            dma((n_wide,)),
-            dma((n_wide,)),
-            dma((n_wide,)),
+            dma((GROUPS, n_wide)),
+            dma((GROUPS, n_wide)),
+            dma((GROUPS, n_wide)),
+            dma((GROUPS, n_wide)),
             dma((4,)),
             dma((4,)),
             dma((2, 2, 3)),

time: 113 us -> 111 us (0.982)
  Pallas kernels: 109 us -> 107 us
    pallas_call x1, Pallas kernels: 43.2 us -> 41.4 us  [flow(): pl.pallas_call(functools.partial(flow_kernel, n_wide, n_narrow), out_shap...]
where the time goes in v3:
time: 111 us
  Pallas kernels  107 us (96%)
  other arithmetic  1.4 us (1%)
  local copies, waits for them, and re-layouts  1.31 us (1%)
    pallas_call x1, Pallas kernels, solve_pressure(): pl.pallas_call(functools.partial(pressure_kernel, n_wide, n_narrow), out_...  53.8 us
    pallas_call x1, Pallas kernels, flow(): pl.pallas_call(functools.partial(flow_kernel, n_wide, n_narrow), out_shap...  41.4 us
    pallas_call x1, Pallas kernels, slab_heat(): pl.pallas_call(gather_kernel, out_shape=jax.ShapeDtypeStruct((lines, 128)...  6.45 us
    pallas_call x1, Pallas kernels, project(): pl.pallas_call(project_kernel, grid=(x_local // planes,), out_shape=[jax....  5.86 us

profile of v3, /device:TPU:1, one launch (start us, length us, event | category | flops | bytes accessed | tf_op | source)
XLA Modules:
  0.0 111.0 jit_solution(3344967464713390195)
XLA Ops:
  0.6 0.7 broadcast_multiply_fusion
  1.3 0.7 add.3.target
  2.0 1.2 %copy-done.1 = f32[16,32,512]{2,1,0:T(8,128)S(1)} copy-done((f32[16,32,512]{2,1,0:T(8,128)S(1)}, f32[16,32,512]{2,1,0:T(8,128)}, u32[]{:S(2)}) %copy-start.1) | copy-done | bytes 1048600
  3.3 41.4 %flow.1 = (f32[3,16,32,512]{3,2,1,0:T(8,128)}, f32[16,32,512]{2,1,0:T(8,128)S(1)}, f32[4,512,128]{2,1,0:T(8,128)S(1)}) custom-call(f32[3,16,32,512]{3,2,1,0:T(8,128)} %vel_in.1, f32[3,16,32,512]{3,2,1,0:T(8,128)} %push_in.1, f32[16,32,512]{2,1,0:T(8,128)S(1)} %copy-done.1), custom_call_target="tpu_custom_call" | custom-call | tf_op jit(solution)/shard_map/flow/pallas_call | solution.py:280
  44.6 0.0 copy-start.2
  44.6 0.0 copy-start.3
  44.6 0.0 copy-start.4
  44.7 0.0 copy-start.5
  44.7 0.0 copy-start.6
  44.7 0.0 copy-start.7
  44.7 0.0 copy-start.8
  44.7 0.0 copy-start.9
  44.7 0.0 copy-start.10
  44.7 0.0 copy-start.11
  44.7 0.0 copy-start.12
  44.8 0.0 copy-start.13
  44.8 6.4 %slab_heat.1 = f32[8192,128]{1,0:T(8,128)S(1)} custom-call(s32[2048]{0:T(1024)S(1)} %add.3.target, f32[4,512,128]{2,1,0:T(8,128)S(1)} %get-tuple-element.10.heat), custom_call_target="tpu_custom_call" | custom-call | tf_op jit(solution)/shard_map/slab_heat/pallas_call | solution.py:322
  51.2 0.0 copy-done.2
  51.2 0.0 copy-done.3
  51.2 0.0 copy-done.4
  51.3 0.0 copy-done.5
  51.3 0.0 copy-done.6
  51.3 0.0 copy-done.7
  51.3 0.0 copy-done.8
  51.3 0.0 copy-done.9
  51.3 0.0 copy-done.10
  51.3 0.0 copy-done.11
  51.3 0.0 copy-done.12
  51.3 0.0 copy-done.13
  51.3 0.0 copy-start
  51.4 53.8 %pressure.1 = (f32[18,32,512]{2,1,0:T(8,128)S(1)}, f32[2,16,512]{2,1,0:T(8,128)S(1)}, f32[22,48,128]{2,1,0:T(8,128)S(1)}, f32[22,48,128]{2,1,0:T(8,128)S(1)}) custom-call(f32[8,2,32,512]{3,2,1,0:T(8,128)S(1)} %bitcast.4, f32[4,4,512,128]{3,2,1,0:T(8,128)S(1)} %bitcast.3, f32[16,32,128]{2,1,0:T(8,128)S(1)} %copy-done.6, f32[16,32,128]{2,1,0:T(8,128)S(1)} %copy-done.7, ...), custom_call_target="tpu_custom_call" | custom-call | tf_op jit(solution)/shard_map/pressure/pallas_call | solution.py:891
  105.1 5.9 %projection.1 = (f32[3,16,32,512]{3,2,1,0:T(8,128)}, f32[16,32,128]{2,1,0:T(8,128)}) custom-call(f32[18,32,512]{2,1,0:T(8,128)S(1)} %get-tuple-element.11.lead.trail, f32[18,32,512]{2,1,0:T(8,128)S(1)} %get-tuple-element.11.lead.trail, f32[2,16,512]{2,1,0:T(8,128)S(1)} %get-tuple-element.12.y_halo, f32[22,48,128]{2,1,0:T(8,128)S(1)} %get-tuple-element.13.tp, ...), custom_call_target="tpu_custom_call" | custom-call | tf_op jit(solution)/shard_map/projection/pallas_call | solution.py:1009
  (2 shorter events, 0.0 us)
Async XLA Ops:
  2.0 1.2 %copy-start.1 = (f32[16,32,512]{2,1,0:T(8,128)S(1)}, f32[16,32,512]{2,1,0:T(8,128)}, u32[]{:S(2)}) copy-start(f32[16,32,512]{2,1,0:T(8,128)} %warmth_in.1) | copy-start | bytes 3145732
  44.6 6.6 %copy-start.2 = (bf16[512,512]{1,0:T(8,128)(2,1)S(1)}, bf16[512,512]{1,0:T(8,128)(2,1)}, u32[]{:S(2)}) copy-start(bf16[512,512]{1,0:T(8,128)(2,1)} %constant.25.clone.rest_3_) | copy-start | bytes 1572868
  44.6 6.6 %copy-start.3 = (bf16[512,512]{1,0:T(8,128)(2,1)S(1)}, bf16[512,512]{1,0:T(8,128)(2,1)}, u32[]{:S(2)}) copy-start(bf16[512,512]{1,0:T(8,128)(2,1)} %constant.24.clone.rest_2_) | copy-start | bytes 1572868
  44.6 6.6 %copy-start.4 = (bf16[512,512]{1,0:T(8,128)(2,1)S(1)}, bf16[512,512]{1,0:T(8,128)(2,1)}, u32[]{:S(2)}) copy-start(bf16[512,512]{1,0:T(8,128)(2,1)} %constant.23.clone.rest_1_) | copy-start | bytes 1572868
  44.7 6.6 %copy-start.5 = (bf16[512,512]{1,0:T(8,128)(2,1)S(1)}, bf16[512,512]{1,0:T(8,128)(2,1)}, u32[]{:S(2)}) copy-start(bf16[512,512]{1,0:T(8,128)(2,1)} %constant.22.clone.rest_0_) | copy-start | bytes 1572868
  44.7 6.6 %copy-start.6 = (f32[16,32,128]{2,1,0:T(8,128)S(1)}, f32[16,32,128]{2,1,0:T(8,128)}, u32[]{:S(2)}) copy-start(f32[16,32,128]{2,1,0:T(8,128)} %substrate.1) | copy-start | bytes 786436
  44.7 6.6 %copy-start.7 = (f32[16,32,128]{2,1,0:T(8,128)S(1)}, f32[16,32,128]{2,1,0:T(8,128)}, u32[]{:S(2)}) copy-start(f32[16,32,128]{2,1,0:T(8,128)} %spread.1) | copy-start | bytes 786436
  44.7 6.6 %copy-start.8 = (f32[256,128]{1,0:T(8,128)S(1)}, f32[256,128]{1,0:T(8,128)}, u32[]{:S(2)}) copy-start(f32[256,128]{1,0:T(8,128)} %constant.30.clone.rest_8_) | copy-start | bytes 393220
  44.7 6.6 %copy-start.9 = (bf16[256,256]{1,0:T(8,128)(2,1)S(1)}, bf16[256,256]{1,0:T(8,128)(2,1)}, u32[]{:S(2)}) copy-start(bf16[256,256]{1,0:T(8,128)(2,1)} %constant.29.clone.rest_7_) | copy-start | bytes 393220
  44.7 6.6 %copy-start.10 = (bf16[256,256]{1,0:T(8,128)(2,1)S(1)}, bf16[256,256]{1,0:T(8,128)(2,1)}, u32[]{:S(2)}) copy-start(bf16[256,256]{1,0:T(8,128)(2,1)} %constant.28.clone.rest_6_) | copy-start | bytes 393220
  44.7 6.6 %copy-start.11 = (bf16[256,256]{1,0:T(8,128)(2,1)S(1)}, bf16[256,256]{1,0:T(8,128)(2,1)}, u32[]{:S(2)}) copy-start(bf16[256,256]{1,0:T(8,128)(2,1)} %constant.27.clone.rest_5_) | copy-start | bytes 393220
  44.7 6.6 %copy-start.12 = (bf16[256,256]{1,0:T(8,128)(2,1)S(1)}, bf16[256,256]{1,0:T(8,128)(2,1)}, u32[]{:S(2)}) copy-start(bf16[256,256]{1,0:T(8,128)(2,1)} %constant.26.clone.rest_4_) | copy-start | bytes 393220
  44.8 6.6 %copy-start.13 = (f32[8,8,128]{2,1,0:T(8,128)S(1)}, f32[8,8,128]{2,1,0:T(8,128)}, u32[]{:S(2)}) copy-start(f32[8,8,128]{2,1,0:T(8,128)} %constant.31.clone.rest_9_) | copy-start | bytes 98308
  51.3 53.8 %copy-start = (f32[3,16,32,512]{3,2,1,0:T(8,128)S(1)}, f32[3,16,32,512]{3,2,1,0:T(8,128)}, u32[]{:S(2)}) copy-start(f32[3,16,32,512]{3,2,1,0:T(8,128)} %get-tuple-element.15.current) | copy-start | bytes 9437188

commit v4 on v3

--- a/solution.py
+++ b/solution.py
@@ -666,30 +666,30 @@
         to = along(k)
         return pltpu.make_async_remote_copy(
             src_ref=mom.at[g, chunk(to)], dst_ref=mrecv.at[g, w],
-            send_sem=wf_send.at[g, k], recv_sem=wf_recv.at[g, k],
+            send_sem=wf_send.at[g], recv_sem=wf_recv.at[g],
             device_id=(to, n), device_id_type=MESH,
         )
 
-    def out_arrival(g, k):
-        here = mrecv.at[g, along(n_wide - k)]
-        return pltpu.make_async_remote_copy(
-            src_ref=here, dst_ref=here, send_sem=wf_send.at[g, k], recv_sem=wf_recv.at[g, k],
-            device_id=(along(n_wide - k), n), device_id_type=MESH,
+    def all_out(g):
+        here = mrecv.at[g, pl.ds(0, n_wide - 1)]
+        return pltpu.make_async_remote_copy(
+            src_ref=here, dst_ref=here, send_sem=wf_send.at[g], recv_sem=wf_recv.at[g],
+            device_id=(along(1), n), device_id_type=MESH,
         )
 
     def back_copy(g, k):
         to = along(k)
         return pltpu.make_async_remote_copy(
             src_ref=absend.at[g, to], dst_ref=ab.at[g, chunk(w)],
-            send_sem=wb_send.at[g, k], recv_sem=wb_recv.at[g, k],
+            send_sem=wb_send.at[g], recv_sem=wb_recv.at[g],
             device_id=(to, n), device_id_type=MESH,
         )
 
-    def back_arrival(g, k):
-        here = ab.at[g, chunk(along(n_wide - k))]
-        return pltpu.make_async_remote_copy(
-            src_ref=here, dst_ref=here, send_sem=wb_send.at[g, k], recv_sem=wb_recv.at[g, k],
-            device_id=(along(n_wide - k), n), device_id_type=MESH,
+    def all_back(g):
+        here = ab.at[g, pl.ds(0, (n_wide - 1) * chunk_rows)]
+        return pltpu.make_async_remote_copy(
+            src_ref=here, dst_ref=here, send_sem=wb_send.at[g], recv_sem=wb_recv.at[g],
+            device_id=(along(1), n), device_id_type=MESH,
         )
 
     def each(count, action):
@@ -734,7 +734,7 @@
     q = power(rtab[0, chunk(w)], xps)
     closing = 1.0 / (1.0 - power(q, n_wide))
     for g in range(GROUPS):
-        each(n_wide, lambda k: out_arrival(g, k).wait_recv())
+        all_out(g).wait_recv()
         f = mrecv[g, 0]
         b = mrecv[g, n_wide - 1]
         for j in range(1, n_wide):
@@ -775,7 +775,7 @@
     loaded(6, 7)
     for g in range(GROUPS):
         span = slice(g * per, (g + 1) * per)
-        each(n_wide, lambda k: back_arrival(g, k).wait_recv())
+        all_back(g).wait_recv()
 
         def solve(i, c):
             here = pl.ds(pl.multiple_of(i * block, block), block)
@@ -862,8 +862,8 @@
     for g in range(GROUPS):
         each(n_narrow, lambda k: forward_copy(g, k).wait_send())
         each(n_narrow, lambda k: backward_copy(g, k).wait_send())
-        each(n_wide, lambda k: out_copy(g, k).wait_send())
-        each(n_wide, lambda k: back_copy(g, k).wait_send())
+        all_out(g).wait_send()
+        all_back(g).wait_send()
     for side in (0, 1):
         x_halo(side).wait()
         y_halo_copy(side).wait()
@@ -924,10 +924,10 @@
             dma((GROUPS, n_narrow)),
             dma((GROUPS, n_narrow)),
             dma((GROUPS, n_narrow)),
-            dma((GROUPS, n_wide)),
-            dma((GROUPS, n_wide)),
-            dma((GROUPS, n_wide)),
-            dma((GROUPS, n_wide)),
+            dma((GROUPS,)),
+            dma((GROUPS,)),
+            dma((GROUPS,)),
+            dma((GROUPS,)),
             dma((4,)),
             dma((4,)),
             dma((2, 2, 3)),

time: 111 us -> 110 us (level)
  no operation moved by 1% of the time
where the time goes in v4:
time: 110 us
  Pallas kernels  106 us (96%)
  other arithmetic  1.4 us (1%)
  local copies, waits for them, and re-layouts  1.31 us (1%)
    pallas_call x1, Pallas kernels, solve_pressure(): pl.pallas_call(functools.partial(pressure_kernel, n_wide, n_narrow), out_...  52.7 us
    pallas_call x1, Pallas kernels, flow(): pl.pallas_call(functools.partial(flow_kernel, n_wide, n_narrow), out_shap...  41.4 us
    pallas_call x1, Pallas kernels, slab_heat(): pl.pallas_call(gather_kernel, out_shape=jax.ShapeDtypeStruct((lines, 128)...  6.45 us
    pallas_call x1, Pallas kernels, project(): pl.pallas_call(project_kernel, grid=(x_local // planes,), out_shape=[jax....  5.86 us

profile of v4, /device:TPU:1, one launch (start us, length us, event | category | flops | bytes accessed | tf_op | source)
XLA Modules:
  0.0 109.9 jit_solution(9637937047544545161)
XLA Ops:
  0.6 0.7 broadcast_multiply_fusion
  1.3 0.7 add.3.target
  2.0 1.2 %copy-done.1 = f32[16,32,512]{2,1,0:T(8,128)S(1)} copy-done((f32[16,32,512]{2,1,0:T(8,128)S(1)}, f32[16,32,512]{2,1,0:T(8,128)}, u32[]{:S(2)}) %copy-start.1) | copy-done | bytes 1048600
  3.3 41.4 %flow.1 = (f32[3,16,32,512]{3,2,1,0:T(8,128)}, f32[16,32,512]{2,1,0:T(8,128)S(1)}, f32[4,512,128]{2,1,0:T(8,128)S(1)}) custom-call(f32[3,16,32,512]{3,2,1,0:T(8,128)} %vel_in.1, f32[3,16,32,512]{3,2,1,0:T(8,128)} %push_in.1, f32[16,32,512]{2,1,0:T(8,128)S(1)} %copy-done.1), custom_call_target="tpu_custom_call" | custom-call | tf_op jit(solution)/shard_map/flow/pallas_call | solution.py:280
  44.6 0.0 copy-start.2
  44.6 0.0 copy-start.3
  44.6 0.0 copy-start.4
  44.7 0.0 copy-start.5
  44.7 0.0 copy-start.6
  44.7 0.0 copy-start.7
  44.7 0.0 copy-start.8
  44.7 0.0 copy-start.9
  44.7 0.0 copy-start.10
  44.7 0.0 copy-start.11
  44.7 0.0 copy-start.12
  44.8 0.0 copy-start.13
  44.8 6.4 %slab_heat.1 = f32[8192,128]{1,0:T(8,128)S(1)} custom-call(s32[2048]{0:T(1024)S(1)} %add.3.target, f32[4,512,128]{2,1,0:T(8,128)S(1)} %get-tuple-element.10.heat), custom_call_target="tpu_custom_call" | custom-call | tf_op jit(solution)/shard_map/slab_heat/pallas_call | solution.py:322
  51.2 0.0 copy-done.2
  51.2 0.0 copy-done.3
  51.2 0.0 copy-done.4
  51.3 0.0 copy-done.5
  51.3 0.0 copy-done.6
  51.3 0.0 copy-done.7
  51.3 0.0 copy-done.8
  51.3 0.0 copy-done.9
  51.3 0.0 copy-done.10
  51.3 0.0 copy-done.11
  51.3 0.0 copy-done.12
  51.3 0.0 copy-done.13
  51.3 0.0 copy-start
  51.4 52.7 %pressure.1 = (f32[18,32,512]{2,1,0:T(8,128)S(1)}, f32[2,16,512]{2,1,0:T(8,128)S(1)}, f32[22,48,128]{2,1,0:T(8,128)S(1)}, f32[22,48,128]{2,1,0:T(8,128)S(1)}) custom-call(f32[8,2,32,512]{3,2,1,0:T(8,128)S(1)} %bitcast.4, f32[4,4,512,128]{3,2,1,0:T(8,128)S(1)} %bitcast.3, f32[16,32,128]{2,1,0:T(8,128)S(1)} %copy-done.6, f32[16,32,128]{2,1,0:T(8,128)S(1)} %copy-done.7, ...), custom_call_target="tpu_custom_call" | custom-call | tf_op jit(solution)/shard_map/pressure/pallas_call | solution.py:891
  104.0 5.9 %projection.1 = (f32[3,16,32,512]{3,2,1,0:T(8,128)}, f32[16,32,128]{2,1,0:T(8,128)}) custom-call(f32[18,32,512]{2,1,0:T(8,128)S(1)} %get-tuple-element.11.lead.trail, f32[18,32,512]{2,1,0:T(8,128)S(1)} %get-tuple-element.11.lead.trail, f32[2,16,512]{2,1,0:T(8,128)S(1)} %get-tuple-element.12.y_halo, f32[22,48,128]{2,1,0:T(8,128)S(1)} %get-tuple-element.13.tp, ...), custom_call_target="tpu_custom_call" | custom-call | tf_op jit(solution)/shard_map/projection/pallas_call | solution.py:1009
  (2 shorter events, 0.0 us)
Async XLA Ops:
  2.0 1.2 %copy-start.1 = (f32[16,32,512]{2,1,0:T(8,128)S(1)}, f32[16,32,512]{2,1,0:T(8,128)}, u32[]{:S(2)}) copy-start(f32[16,32,512]{2,1,0:T(8,128)} %warmth_in.1) | copy-start | bytes 3145732
  44.6 6.6 %copy-start.2 = (bf16[512,512]{1,0:T(8,128)(2,1)S(1)}, bf16[512,512]{1,0:T(8,128)(2,1)}, u32[]{:S(2)}) copy-start(bf16[512,512]{1,0:T(8,128)(2,1)} %constant.25.clone.rest_3_) | copy-start | bytes 1572868
  44.6 6.6 %copy-start.3 = (bf16[512,512]{1,0:T(8,128)(2,1)S(1)}, bf16[512,512]{1,0:T(8,128)(2,1)}, u32[]{:S(2)}) copy-start(bf16[512,512]{1,0:T(8,128)(2,1)} %constant.24.clone.rest_2_) | copy-start | bytes 1572868
  44.6 6.6 %copy-start.4 = (bf16[512,512]{1,0:T(8,128)(2,1)S(1)}, bf16[512,512]{1,0:T(8,128)(2,1)}, u32[]{:S(2)}) copy-start(bf16[512,512]{1,0:T(8,128)(2,1)} %constant.23.clone.rest_1_) | copy-start | bytes 1572868
  44.7 6.6 %copy-start.5 = (bf16[512,512]{1,0:T(8,128)(2,1)S(1)}, bf16[512,512]{1,0:T(8,128)(2,1)}, u32[]{:S(2)}) copy-start(bf16[512,512]{1,0:T(8,128)(2,1)} %constant.22.clone.rest_0_) | copy-start | bytes 1572868
  44.7 6.6 %copy-start.6 = (f32[16,32,128]{2,1,0:T(8,128)S(1)}, f32[16,32,128]{2,1,0:T(8,128)}, u32[]{:S(2)}) copy-start(f32[16,32,128]{2,1,0:T(8,128)} %substrate.1) | copy-start | bytes 786436
  44.7 6.6 %copy-start.7 = (f32[16,32,128]{2,1,0:T(8,128)S(1)}, f32[16,32,128]{2,1,0:T(8,128)}, u32[]{:S(2)}) copy-start(f32[16,32,128]{2,1,0:T(8,128)} %spread.1) | copy-start | bytes 786436
  44.7 6.6 %copy-start.8 = (f32[256,128]{1,0:T(8,128)S(1)}, f32[256,128]{1,0:T(8,128)}, u32[]{:S(2)}) copy-start(f32[256,128]{1,0:T(8,128)} %constant.30.clone.rest_8_) | copy-start | bytes 393220
  44.7 6.6 %copy-start.9 = (bf16[256,256]{1,0:T(8,128)(2,1)S(1)}, bf16[256,256]{1,0:T(8,128)(2,1)}, u32[]{:S(2)}) copy-start(bf16[256,256]{1,0:T(8,128)(2,1)} %constant.29.clone.rest_7_) | copy-start | bytes 393220
  44.7 6.6 %copy-start.10 = (bf16[256,256]{1,0:T(8,128)(2,1)S(1)}, bf16[256,256]{1,0:T(8,128)(2,1)}, u32[]{:S(2)}) copy-start(bf16[256,256]{1,0:T(8,128)(2,1)} %constant.28.clone.rest_6_) | copy-start | bytes 393220
  44.7 6.6 %copy-start.11 = (bf16[256,256]{1,0:T(8,128)(2,1)S(1)}, bf16[256,256]{1,0:T(8,128)(2,1)}, u32[]{:S(2)}) copy-start(bf16[256,256]{1,0:T(8,128)(2,1)} %constant.27.clone.rest_5_) | copy-start | bytes 393220
  44.7 6.6 %copy-start.12 = (bf16[256,256]{1,0:T(8,128)(2,1)S(1)}, bf16[256,256]{1,0:T(8,128)(2,1)}, u32[]{:S(2)}) copy-start(bf16[256,256]{1,0:T(8,128)(2,1)} %constant.26.clone.rest_4_) | copy-start | bytes 393220
  44.8 6.6 %copy-start.13 = (f32[8,8,128]{2,1,0:T(8,128)S(1)}, f32[8,8,128]{2,1,0:T(8,128)}, u32[]{:S(2)}) copy-start(f32[8,8,128]{2,1,0:T(8,128)} %constant.31.clone.rest_9_) | copy-start | bytes 98308
  51.3 52.7 %copy-start = (f32[3,16,32,512]{3,2,1,0:T(8,128)S(1)}, f32[3,16,32,512]{3,2,1,0:T(8,128)}, u32[]{:S(2)}) copy-start(f32[3,16,32,512]{3,2,1,0:T(8,128)} %get-tuple-element.15.current) | copy-start | bytes 9437188

commit v5 on v4

--- a/solution.py
+++ b/solution.py
@@ -125,7 +125,7 @@
     def zener_log(x):
         lz[x] = (zener_energy / stress_exponent) * (1.0 / warmth_in[x] - 1.0)
 
-    all_x(zener_log)
+    all_x(zener_log, unroll=2)
     loads[1].wait()
 
     def excess(src, x, r):
@@ -307,7 +307,7 @@
             into[row] = into[row] + heat[m, pl.ds(i, 1)]
         return c
 
-    lax.fori_loop(0, heat.shape[1], cell, 0, unroll=4)
+    lax.fori_loop(0, heat.shape[1], cell, 0, unroll=8)
     step = 256
 
     def join(i, c):
@@ -725,7 +725,7 @@
             mom[g, here] = jnp.where(later_half(block), f + rp * swap(f), b + rp * swap(b))
             return c
 
-        lax.fori_loop(0, n_y // block, moments, 0)
+        lax.fori_loop(0, n_y // block, moments, 0, unroll=2)
         each(n_wide, lambda k: out_copy(g, k).start())
         mrecv[g, w] = mom[g, chunk(w)]
         if g == 0:
@@ -799,7 +799,7 @@
                 ubuf[g * per + k, here] = scale * (f + behind[per - 1 - k])
             return c
 
-        lax.fori_loop(0, n_y // block, solve, 0)
+        lax.fori_loop(0, n_y // block, solve, 0, unroll=2)
         lines = jnp.concatenate([ubuf[i] for i in range(g * per, (g + 1) * per)], axis=1)
         lines = dot_right(iy_h[...], iy_l[...], lines)
         for to in range(n_narrow):

time: 110 us -> 110 us (level)
  no operation moved by 1% of the time
where the time goes in v5:
time: 110 us
  Pallas kernels  106 us (96%)
  other arithmetic  1.4 us (1%)
  local copies, waits for them, and re-layouts  1.31 us (1%)
    pallas_call x1, Pallas kernels, solve_pressure(): pl.pallas_call(functools.partial(pressure_kernel, n_wide, n_narrow), out_...  52.1 us
    pallas_call x1, Pallas kernels, flow(): pl.pallas_call(functools.partial(flow_kernel, n_wide, n_narrow), out_shap...  41.4 us
    pallas_call x1, Pallas kernels, slab_heat(): pl.pallas_call(gather_kernel, out_shape=jax.ShapeDtypeStruct((lines, 128)...  6.78 us
    pallas_call x1, Pallas kernels, project(): pl.pallas_call(project_kernel, grid=(x_local // planes,), out_shape=[jax....  5.86 us

profile of v5, /device:TPU:1, one launch (start us, length us, event | category | flops | bytes accessed | tf_op | source)
XLA Modules:
  0.0 109.6 jit_solution(17062150140098829351)
XLA Ops:
  0.6 0.7 broadcast_multiply_fusion
  1.3 0.7 add.3.target
  2.0 1.2 %copy-done.1 = f32[16,32,512]{2,1,0:T(8,128)S(1)} copy-done((f32[16,32,512]{2,1,0:T(8,128)S(1)}, f32[16,32,512]{2,1,0:T(8,128)}, u32[]{:S(2)}) %copy-start.1) | copy-done | bytes 1048600
  3.3 41.4 %flow.1 = (f32[3,16,32,512]{3,2,1,0:T(8,128)}, f32[16,32,512]{2,1,0:T(8,128)S(1)}, f32[4,512,128]{2,1,0:T(8,128)S(1)}) custom-call(f32[3,16,32,512]{3,2,1,0:T(8,128)} %vel_in.1, f32[3,16,32,512]{3,2,1,0:T(8,128)} %push_in.1, f32[16,32,512]{2,1,0:T(8,128)S(1)} %copy-done.1), custom_call_target="tpu_custom_call" | custom-call | tf_op jit(solution)/shard_map/flow/pallas_call | solution.py:280
  44.6 0.0 copy-start.2
  44.6 0.0 copy-start.3
  44.6 0.0 copy-start.4
  44.7 0.0 copy-start.5
  44.7 0.0 copy-start.6
  44.7 0.0 copy-start.7
  44.7 0.0 copy-start.8
  44.7 0.0 copy-start.9
  44.7 0.0 copy-start.10
  44.7 0.0 copy-start.11
  44.7 0.0 copy-start.12
  44.8 0.0 copy-start.13
  44.8 6.8 %slab_heat.1 = f32[8192,128]{1,0:T(8,128)S(1)} custom-call(s32[2048]{0:T(1024)S(1)} %add.3.target, f32[4,512,128]{2,1,0:T(8,128)S(1)} %get-tuple-element.10.heat), custom_call_target="tpu_custom_call" | custom-call | tf_op jit(solution)/shard_map/slab_heat/pallas_call | solution.py:322
  51.6 0.0 copy-done.2
  51.6 0.0 copy-done.3
  51.6 0.0 copy-done.4
  51.6 0.0 copy-done.5
  51.6 0.0 copy-done.6
  51.6 0.0 copy-done.7
  51.6 0.0 copy-done.8
  51.6 0.0 copy-done.9
  51.6 0.0 copy-done.10
  51.7 0.0 copy-done.11
  51.7 0.0 copy-done.12
  51.7 0.0 copy-done.13
  51.7 0.0 copy-start
  51.7 52.1 %pressure.1 = (f32[18,32,512]{2,1,0:T(8,128)S(1)}, f32[2,16,512]{2,1,0:T(8,128)S(1)}, f32[22,48,128]{2,1,0:T(8,128)S(1)}, f32[22,48,128]{2,1,0:T(8,128)S(1)}) custom-call(f32[8,2,32,512]{3,2,1,0:T(8,128)S(1)} %bitcast.4, f32[4,4,512,128]{3,2,1,0:T(8,128)S(1)} %bitcast.3, f32[16,32,128]{2,1,0:T(8,128)S(1)} %copy-done.6, f32[16,32,128]{2,1,0:T(8,128)S(1)} %copy-done.7, ...), custom_call_target="tpu_custom_call" | custom-call | tf_op jit(solution)/shard_map/pressure/pallas_call | solution.py:891
  103.8 5.9 %projection.1 = (f32[3,16,32,512]{3,2,1,0:T(8,128)}, f32[16,32,128]{2,1,0:T(8,128)}) custom-call(f32[18,32,512]{2,1,0:T(8,128)S(1)} %get-tuple-element.11.lead.trail, f32[18,32,512]{2,1,0:T(8,128)S(1)} %get-tuple-element.11.lead.trail, f32[2,16,512]{2,1,0:T(8,128)S(1)} %get-tuple-element.12.y_halo, f32[22,48,128]{2,1,0:T(8,128)S(1)} %get-tuple-element.13.tp, ...), custom_call_target="tpu_custom_call" | custom-call | tf_op jit(solution)/shard_map/projection/pallas_call | solution.py:1009
  (2 shorter events, 0.0 us)
Async XLA Ops:
  2.0 1.2 %copy-start.1 = (f32[16,32,512]{2,1,0:T(8,128)S(1)}, f32[16,32,512]{2,1,0:T(8,128)}, u32[]{:S(2)}) copy-start(f32[16,32,512]{2,1,0:T(8,128)} %warmth_in.1) | copy-start | bytes 3145732
  44.6 6.9 %copy-start.2 = (bf16[512,512]{1,0:T(8,128)(2,1)S(1)}, bf16[512,512]{1,0:T(8,128)(2,1)}, u32[]{:S(2)}) copy-start(bf16[512,512]{1,0:T(8,128)(2,1)} %constant.25.clone.rest_3_) | copy-start | bytes 1572868
  44.6 6.9 %copy-start.3 = (bf16[512,512]{1,0:T(8,128)(2,1)S(1)}, bf16[512,512]{1,0:T(8,128)(2,1)}, u32[]{:S(2)}) copy-start(bf16[512,512]{1,0:T(8,128)(2,1)} %constant.24.clone.rest_2_) | copy-start | bytes 1572868
  44.6 6.9 %copy-start.4 = (bf16[512,512]{1,0:T(8,128)(2,1)S(1)}, bf16[512,512]{1,0:T(8,128)(2,1)}, u32[]{:S(2)}) copy-start(bf16[512,512]{1,0:T(8,128)(2,1)} %constant.23.clone.rest_1_) | copy-start | bytes 1572868
  44.7 6.9 %copy-start.5 = (bf16[512,512]{1,0:T(8,128)(2,1)S(1)}, bf16[512,512]{1,0:T(8,128)(2,1)}, u32[]{:S(2)}) copy-start(bf16[512,512]{1,0:T(8,128)(2,1)} %constant.22.clone.rest_0_) | copy-start | bytes 1572868
  44.7 6.9 %copy-start.6 = (f32[16,32,128]{2,1,0:T(8,128)S(1)}, f32[16,32,128]{2,1,0:T(8,128)}, u32[]{:S(2)}) copy-start(f32[16,32,128]{2,1,0:T(8,128)} %substrate.1) | copy-start | bytes 786436
  44.7 6.9 %copy-start.7 = (f32[16,32,128]{2,1,0:T(8,128)S(1)}, f32[16,32,128]{2,1,0:T(8,128)}, u32[]{:S(2)}) copy-start(f32[16,32,128]{2,1,0:T(8,128)} %spread.1) | copy-start | bytes 786436
  44.7 6.9 %copy-start.8 = (f32[256,128]{1,0:T(8,128)S(1)}, f32[256,128]{1,0:T(8,128)}, u32[]{:S(2)}) copy-start(f32[256,128]{1,0:T(8,128)} %constant.30.clone.rest_8_) | copy-start | bytes 393220
  44.7 6.9 %copy-start.9 = (bf16[256,256]{1,0:T(8,128)(2,1)S(1)}, bf16[256,256]{1,0:T(8,128)(2,1)}, u32[]{:S(2)}) copy-start(bf16[256,256]{1,0:T(8,128)(2,1)} %constant.29.clone.rest_7_) | copy-start | bytes 393220
  44.7 6.9 %copy-start.10 = (bf16[256,256]{1,0:T(8,128)(2,1)S(1)}, bf16[256,256]{1,0:T(8,128)(2,1)}, u32[]{:S(2)}) copy-start(bf16[256,256]{1,0:T(8,128)(2,1)} %constant.28.clone.rest_6_) | copy-start | bytes 393220
  44.7 6.9 %copy-start.11 = (bf16[256,256]{1,0:T(8,128)(2,1)S(1)}, bf16[256,256]{1,0:T(8,128)(2,1)}, u32[]{:S(2)}) copy-start(bf16[256,256]{1,0:T(8,128)(2,1)} %constant.27.clone.rest_5_) | copy-start | bytes 393220
  44.7 6.9 %copy-start.12 = (bf16[256,256]{1,0:T(8,128)(2,1)S(1)}, bf16[256,256]{1,0:T(8,128)(2,1)}, u32[]{:S(2)}) copy-start(bf16[256,256]{1,0:T(8,128)(2,1)} %constant.26.clone.rest_4_) | copy-start | bytes 393220
  44.8 6.9 %copy-start.13 = (f32[8,8,128]{2,1,0:T(8,128)S(1)}, f32[8,8,128]{2,1,0:T(8,128)}, u32[]{:S(2)}) copy-start(f32[8,8,128]{2,1,0:T(8,128)} %constant.31.clone.rest_9_) | copy-start | bytes 98308
  51.7 52.1 %copy-start = (f32[3,16,32,512]{3,2,1,0:T(8,128)S(1)}, f32[3,16,32,512]{3,2,1,0:T(8,128)}, u32[]{:S(2)}) copy-start(f32[3,16,32,512]{3,2,1,0:T(8,128)} %get-tuple-element.15.current) | copy-start | bytes 9437188
